TPU v7x, 32 devices: a whole 2x2x4 slice. The times are simulated.
32 devices in a mesh: rhs: 8 (over z, x), clus: 4 (over y, core).
Axes of the slice: x: 2, y: 2, z: 4, core: 2. Of those that a mesh axis runs over, the one named last changes fastest.
Arguments:
- incident: bfloat16 [832, 32768], P('rhs', 'clus'), may hold values from -6 to 6
- v_factors: bfloat16 [20, 2048, 128], P('clus', 'rhs'), may hold values from -0.125 to 0.125
- u_factors: bfloat16 [40, 2048, 128], P('clus', 'rhs'), may hold values from -0.5 to 0.5
- block_source: int32 [20], P('clus'), may hold values from 0 to 3
- block_rank: int32 [20], P('clus'), may hold values from 16 to 128
- block_slot: int32 [20], P('clus'), may hold values from 0 to 39, as said below
- slot_target: int32 [40], P('clus'), may hold values from 0 to 3
Outputs:
- scattered: bfloat16 [832, 32768], P('rhs', 'clus')
Inputs may be any that keep to these rules, and one draw needn't show every extreme that they name: `block_slot`: every value is a slot number, all 20 values are distinct, and slot v belongs to index v // 10 of clus. The 5 blocks of one index of clus name at most 3 slots of any one index, and in every draw some index sends exactly 3 to one index and some index of clus receives exactly 10 blocks. Which slots stay empty varies.
All inputs are finite; a program needn't handle non-finite values.
Results may differ from a plain program's by a relative error of at most 0.0049.
Values may be sent and summed in bfloat16 or wider, within the bound.
No kernel may reach another device: no remote copies, remote signals or barrier semaphores. Data moves between devices by JAX's collectives and lax.ppermute only.
A program may use at most 64 MiB of HBM per device.

v0:
```python
import functools

import jax
import jax.numpy as jnp
from jax import lax
from jax.experimental import pallas as pl
from jax.experimental.pallas import tpu as pltpu
from jax.sharding import PartitionSpec as P

VMEM = pl.BlockSpec(memory_space=pltpu.VMEM)
SMEM = pl.BlockSpec(memory_space=pltpu.SMEM)
LIMIT = 10 * 1024 * 1024


def call(body, out_shape, in_specs, name, flops=0, moved=0, scratch=()):
    out_specs = [VMEM] * len(out_shape) if isinstance(out_shape, list) else VMEM
    return pl.pallas_call(
        body,
        out_shape=out_shape,
        in_specs=in_specs,
        out_specs=out_specs,
        scratch_shapes=list(scratch),
        compiler_params=pltpu.CompilerParams(vmem_limit_bytes=LIMIT),
        cost_estimate=pl.CostEstimate(flops=flops, bytes_accessed=moved, transcendentals=0),
        name=name,
    )


def pack_body(seg, pos_ref, x_ref, *out_refs):
    half, piece = 1 - pos_ref[0], 0
    for out_ref in out_refs:
        for place in range(0, out_ref.shape[1], seg):
            start = pl.multiple_of((2 * piece + half) * seg, seg)
            out_ref[:, place : place + seg] = x_ref[:, pl.ds(start, seg)]
            piece += 1


def compress_body(seg, pos_ref, source_ref, x_ref, xl_ref, xh_ref, *refs):
    v0, v1, v2, v3, v4, out_ref, send_ref, xn_ref = refs
    half, mine = pos_ref[0], pos_ref[1]
    columns = x_ref.shape[0]
    xn_ref[:, : xl_ref.shape[1]] = xl_ref[...]
    xn_ref[:, xl_ref.shape[1] :] = xh_ref[...]
    out_ref[...] = jnp.zeros_like(out_ref)

    def run(shards):
        for block in range(out_ref.shape[0]):
            source = source_ref[block]
            own = other = 0.0
            for step, shard in enumerate(shards):
                piece = source * PLACES + jnp.bitwise_xor(mine, step)
                here = pl.multiple_of((piece * 2 + half) * seg, seg)
                there = pl.multiple_of(piece * seg, seg)
                rows = shard[block]
                own += jnp.dot(x_ref[:, pl.ds(here, seg)], rows, preferred_element_type=jnp.float32)
                other += jnp.dot(
                    xn_ref[:, pl.ds(there, seg)], rows, preferred_element_type=jnp.float32
                )
            out_ref[block, half, :columns] = own
            out_ref[block, 1 - half, :columns] = other

    inner = (mine == 1) | (mine == 2)

    @pl.when(inner)
    def _():
        run((v0, v1, v2, v3))

    @pl.when(jnp.logical_not(inner))
    def _():
        run((v0, v1, v2, v4))

    send_ref[...] = out_ref[...].astype(send_ref.dtype)


def place_columns(value, offset, store):
    width = value.shape[-1]
    shift = lax.rem(offset, width)
    turned = pltpu.roll(value, shift, value.ndim - 1)
    lane = lax.broadcasted_iota(jnp.int32, value.shape, value.ndim - 1)
    store(offset // width, jnp.where(lane >= shift, turned, 0.0))
    store(offset // width + 1, jnp.where(lane < shift, turned, 0.0))


def squeeze_body(offset_ref, used_ref, u_ref, out_ref, acc):
    acc[...] = jnp.zeros_like(acc)
    for slot in range(u_ref.shape[0]):
        value = u_ref[slot].astype(jnp.float32)
        lane = lax.broadcasted_iota(jnp.int32, value.shape, 1)

        def store(tile, part):
            acc[tile] += part

        place_columns(jnp.where(lane < used_ref[slot], value, 0.0), offset_ref[slot], store)
    out_ref[...] = acc[: out_ref.shape[0]].astype(out_ref.dtype)


def land_body(index_ref, target_ref, offset_ref, comp_ref, rows_ref):
    rows_ref[...] = jnp.zeros_like(rows_ref)
    last = rows_ref.shape[0] - 1
    for slot in range(index_ref.shape[0]):
        block, target = index_ref[slot], target_ref[slot]
        value = comp_ref[jnp.maximum(block, 0)].astype(jnp.float32)
        value = jnp.where(block >= 0, value, 0.0).reshape(rows_ref.shape[2:])

        def store(tile, part):
            rows_ref[jnp.minimum(tile, last), target] += part.astype(rows_ref.dtype)

        place_columns(value, offset_ref[slot], store)


def lined_up(ref, rows):
    return jnp.concatenate([ref[tile].reshape(rows, ref.shape[-1]) for tile in range(ref.shape[0])], axis=1)


def expand_body(seg, columns, pos_ref, rows_ref, *refs):
    own_ref, other_ref, acc = refs[-3:]
    half, mine = pos_ref[0], pos_ref[1]
    clusters, sides, padded = acc.shape[:3]

    def run(shard):
        product = lax.dot_general(
            lined_up(rows_ref, clusters * sides * padded),
            lined_up(shard, seg),
            (((1,), (1,)), ((), ())),
            preferred_element_type=jnp.float32,
        )
        acc[...] = product.reshape(acc.shape)

    if len(refs) == 4:
        run(refs[0])
    else:
        inner = (mine == 1) | (mine == 2)

        @pl.when(inner)
        def _():
            run(refs[0])

        @pl.when(jnp.logical_not(inner))
        def _():
            run(refs[1])

    for target in range(clusters):
        span = slice(target * seg, (target + 1) * seg)
        own_ref[:, span] = acc[target, half, :columns].astype(own_ref.dtype)
        other_ref[:, span] = acc[target, 1 - half, :columns].astype(other_ref.dtype)


def expand_own_body(seg, columns, pos_ref, rows_ref, u_ref, side_ref, out_ref, acc):
    half = pos_ref[0]
    clusters, padded = acc.shape[:2]
    start = pl.multiple_of(half * padded, padded)
    tiles = [
        rows_ref[tile, :, pl.ds(start, padded)].reshape(clusters * padded, rows_ref.shape[3])
        for tile in range(rows_ref.shape[0])
    ]
    rows = jnp.concatenate(tiles, axis=1)
    for shard, place in ((u_ref, half), (side_ref, 1 - half)):
        product = lax.dot_general(
            rows,
            lined_up(shard, seg),
            (((1,), (1,)), ((), ())),
            preferred_element_type=jnp.float32,
        )
        acc[...] = product.reshape(acc.shape)
        for target in range(clusters):
            start = pl.multiple_of((2 * target + place) * seg, seg)
            out_ref[:, pl.ds(start, seg)] = acc[target, :columns].astype(out_ref.dtype)


def join_body(seg, clusters, pos_ref, first_ref, *refs):
    out_ref = refs[-1]
    half, mine = pos_ref[0], pos_ref[1]
    for target in range(clusters):
        start = pl.multiple_of((target * PLACES + mine) * 2 * seg, 2 * seg)
        span = slice(2 * target * seg, 2 * (target + 1) * seg)
        out_ref[:, pl.ds(start, 2 * seg)] = first_ref[:, span]
    for step in range(1, PLACES):
        place = jnp.bitwise_xor(mine, step)
        for target in range(clusters):
            span = slice(target * seg, (target + 1) * seg)
            base = (target * PLACES + place) * 2
            here = pl.multiple_of((base + half) * seg, seg)
            there = pl.multiple_of((base + 1 - half) * seg, seg)
            out_ref[:, pl.ds(here, seg)] = refs[step - 1][:, span]
            out_ref[:, pl.ds(there, seg)] = refs[PLACES + step - 2][:, span]


def after(value, *first):
    return lax.optimization_barrier((value, *first))[0]


PLACES = 4


def paired(incident, v_factors, u_factors, block_source, block_rank, block_slot, slot_target):
    columns, width = incident.shape
    padded = -(-columns // 16) * 16
    blocks, seg, rank_max = v_factors.shape
    capacity = u_factors.shape[0]
    owners = lax.axis_size("clus")
    clusters = width // (seg * 2 * PLACES)
    me, owner = lax.axis_index("rhs"), lax.axis_index("clus")
    position = jnp.stack([me % 2, me // 2]).astype(jnp.int32)

    def move(array, pairs):
        return lax.ppermute(array, "rhs", [(2 * a + i, 2 * b + i) for a, b in pairs for i in (0, 1)])

    def across(array):
        return lax.ppermute(array, "rhs", [(p, p ^ 1) for p in range(2 * PLACES)])

    far = [(p, p ^ 2) for p in range(PLACES)]
    near = [(p, p ^ 1) for p in range(PLACES)]
    middle = [(1, 2), (2, 1)]
    ends = [(1, 0), (2, 3)]

    stages = [1 << bit for bit in reversed(range((owners - 1).bit_length()))]

    def swapped(array, stage):
        return lax.ppermute(array, "clus", [(p, p ^ stage) for p in range(owners)])

    def double(array, stage):
        return jnp.concatenate([array, swapped(array, stage)], axis=0)

    v_far, v_near = move(v_factors, far), move(v_factors, near)
    packed = call(
        functools.partial(pack_body, seg),
        [
            jax.ShapeDtypeStruct((columns, count * PLACES * seg), incident.dtype)
            for count in (clusters // 2, clusters - clusters // 2)
        ],
        [SMEM, VMEM],
        "pack",
        moved=3 * columns * width,
    )(position, incident)
    table = jnp.stack([block_slot, block_rank], axis=1)
    for stage in stages:
        table = double(table, stage)
    slots, ranks = table[:, 0], table[:, 1]
    wanted = owner * capacity + lax.broadcasted_iota(jnp.int32, (capacity, slots.shape[0]), 0)
    order = lax.broadcasted_iota(jnp.int32, (capacity, slots.shape[0]), 1)
    found = wanted == slots[None, :]
    feeding = jnp.max(jnp.where(found, order, -1), axis=1)
    used = jnp.sum(jnp.where(found, ranks[None, :], 0), axis=1)
    earlier = lax.broadcasted_iota(jnp.int32, (capacity, capacity), 1)
    earlier = earlier < lax.broadcasted_iota(jnp.int32, (capacity, capacity), 0)
    offset = jnp.sum(jnp.where(earlier, used[None, :], 0), axis=1)
    place = lax.broadcasted_iota(jnp.int32, (owners, slots.shape[0]), 0)
    held = (slots[None, :] >= place * capacity) & (slots[None, :] < (place + 1) * capacity)
    fullest = jnp.max(jnp.sum(jnp.where(held, ranks[None, :], 0), axis=1))
    tiles = sorted({-(-capacity * part // 10) for part in (5, 6, 7, 8, 10)})
    level = sum((fullest > count * rank_max).astype(jnp.int32) for count in tiles[:-1])
    squeezed = call(
        squeeze_body,
        jax.ShapeDtypeStruct(u_factors.shape, u_factors.dtype),
        [SMEM, SMEM, VMEM],
        "squeeze",
        moved=4 * u_factors.size,
        scratch=[pltpu.VMEM((capacity + 2, seg, rank_max), jnp.float32)],
    )(offset, used, u_factors)

    x_low, x_high = [across(part) for part in packed]
    v_ends = move(after(v_far, *packed), ends)
    v_middle = move(after(v_factors, v_far), middle)
    arrived = lax.optimization_barrier(
        (x_low, x_high, v_near, v_far, v_middle, v_ends, squeezed, level)
    )

    def rest(count, x_low, x_high, v_near, v_far, v_middle, v_ends, squeezed):
        target_factors = squeezed[:count]
        u_far, u_near = move(target_factors, far), move(target_factors, near)
        partial, sent = call(
            functools.partial(compress_body, seg),
            [
                jax.ShapeDtypeStruct((blocks, 2, padded, rank_max), jnp.float32),
                jax.ShapeDtypeStruct((blocks, 2, padded, rank_max), jnp.bfloat16),
            ],
            [SMEM, SMEM] + [VMEM] * 8,
            "compress",
            flops=4 * blocks * columns * seg * PLACES * rank_max,
            moved=3 * columns * width + 2 * PLACES * v_factors.size,
            scratch=[pltpu.VMEM((columns, width // 2), incident.dtype)],
        )(
            position, block_source, incident, x_low, x_high,
            v_factors, v_near, v_far, v_middle, v_ends,
        )
        received = across(sent)
        u_side = across(after(target_factors, received))
        rank_index = lax.broadcasted_iota(jnp.int32, (blocks, 1, 1, rank_max), 3)
        rows = jnp.where(
            rank_index < block_rank[:, None, None, None],
            partial + received.astype(jnp.float32),
            0.0,
        ).astype(jnp.bfloat16)

        rounds, gathered = 1 + jnp.minimum(me, 0), rows
        for stage in stages:
            other = lax.fori_loop(
                0, rounds, lambda _, array, stage=stage: swapped(array, stage), gathered
            )
            gathered = jnp.concatenate([gathered, other], axis=0)
        u_ends = move(after(u_far, gathered), ends)
        u_middle = move(after(target_factors, u_far, gathered), middle)
        slot_rows = call(
            land_body,
            jax.ShapeDtypeStruct((count, clusters, 2 * padded, rank_max), jnp.bfloat16),
            [SMEM, SMEM, SMEM, VMEM],
            "land",
            moved=2 * gathered.size * (1 + clusters),
        )(feeding, slot_target, offset, gathered)

        chunk = jax.ShapeDtypeStruct((columns, clusters * seg), jnp.bfloat16)
        own_parts, other_parts = [None] * PLACES, [None] * PLACES
        work = 4 * clusters * count * columns * seg * rank_max
        first = call(
            functools.partial(expand_own_body, seg, columns),
            jax.ShapeDtypeStruct((columns, 2 * clusters * seg), jnp.bfloat16),
            [SMEM] + [VMEM] * 3,
            "expand_own",
            flops=work,
            moved=4 * target_factors.size + 2 * slot_rows.size + 4 * columns * clusters * seg,
            scratch=[pltpu.VMEM((clusters, padded, seg), jnp.float32)],
        )(position, slot_rows, target_factors, u_side)
        finished = []
        for step, shards in ((1, [u_near]), (2, [u_far]), (3, [u_middle, u_ends])):
            if finished:
                slot_rows = after(slot_rows, own_parts[finished[-1]])
            if len(finished) == 2:
                slot_rows = after(slot_rows, first, other_parts[finished[0]])
            own, other = call(
                functools.partial(expand_body, seg, columns),
                [chunk, chunk],
                [SMEM, VMEM] + [VMEM] * len(shards),
                "expand",
                flops=work,
                moved=2 * target_factors.size + 2 * slot_rows.size + 4 * columns * clusters * seg,
                scratch=[pltpu.VMEM((clusters, 2, padded, seg), jnp.float32)],
            )(position, slot_rows, *shards)
            own_parts[step], other_parts[step] = own, across(other)
            finished.append(step)
        return call(
            functools.partial(join_body, seg, clusters),
            jax.ShapeDtypeStruct((columns, width), jnp.bfloat16),
            [SMEM] + [VMEM] * (2 * PLACES - 1),
            "join",
            moved=4 * columns * width,
        )(position, first, *own_parts[1:], *other_parts[1:])

    return lax.switch(
        arrived[-1], [functools.partial(rest, count) for count in tiles], *arrived[:-1]
    )


def gathered_plan(
    incident, v_factors, u_factors, block_source, block_rank, block_slot, slot_target
):
    columns = incident.shape[0]
    blocks = v_factors.shape[0]
    rank_max = v_factors.shape[2]
    capacity = u_factors.shape[0]
    devices = lax.axis_size("clus")
    cluster_len = v_factors.shape[1] * lax.axis_size("rhs")
    local_clusters = incident.shape[1] // cluster_len
    per_peer = max(1, (2 * blocks + devices - 1) // devices)
    sources = jnp.take(incident.reshape(columns, local_clusters, cluster_len), block_source, axis=1)
    compressed = jnp.einsum(
        "cbr,brk->bck",
        sources,
        lax.all_gather(v_factors, "rhs", axis=1, tiled=True),
        preferred_element_type=jnp.float32,
    )
    rank_index = lax.broadcasted_iota(jnp.int32, (blocks, 1, rank_max), 2)
    compressed = jnp.where(rank_index < block_rank[:, None, None], compressed, 0.0).astype(
        jnp.bfloat16
    )
    target_dev = block_slot // capacity
    target_pos = block_slot % capacity
    later_index = lax.broadcasted_iota(jnp.int32, (blocks, blocks), 0)
    earlier_index = lax.broadcasted_iota(jnp.int32, (blocks, blocks), 1)
    same_target = target_dev[None, :] == target_dev[:, None]
    before = jnp.sum((same_target & (earlier_index < later_index)).astype(jnp.int32), axis=1)
    position = target_dev * per_peer + before
    places = lax.broadcasted_iota(jnp.int32, (blocks, devices * per_peer), 1)
    placed = position[:, None] == places
    outgoing = jnp.einsum(
        "bp,bck->pck", placed.astype(jnp.bfloat16), compressed, preferred_element_type=jnp.float32
    ).astype(jnp.bfloat16)
    labels = jnp.sum(jnp.where(placed, target_pos[:, None] + 1, 0), axis=0) - 1
    arrived, arrived_labels = (
        lax.all_to_all(outgoing, "clus", split_axis=0, concat_axis=0, tiled=True),
        lax.all_to_all(labels, "clus", split_axis=0, concat_axis=0, tiled=True),
    )
    slot_ids = lax.broadcasted_iota(jnp.int32, (devices * per_peer, capacity), 1)
    landing = (arrived_labels[:, None] == slot_ids).astype(jnp.bfloat16)
    slot_rows = jnp.einsum(
        "pj,pck->jck", landing, arrived, preferred_element_type=jnp.float32
    ).astype(jnp.bfloat16)
    cluster_ids = lax.broadcasted_iota(jnp.int32, (capacity, local_clusters), 1)
    owners = (slot_target[:, None] == cluster_ids).astype(jnp.float32)
    products = jnp.einsum(
        "jck,jrk->jcr",
        slot_rows,
        lax.all_gather(u_factors, "rhs", axis=1, tiled=True),
        preferred_element_type=jnp.float32,
    )
    summed = jnp.einsum("jt,jcr->ctr", owners, products, precision=lax.Precision.HIGHEST)
    return summed.reshape(columns, local_clusters * cluster_len).astype(jnp.bfloat16)


def local(incident, v_factors, *rest):
    owners = lax.axis_size("clus")
    fits = (
        lax.axis_size("rhs") == 2 * PLACES
        and v_factors.shape[1] % 128 == 0
        and owners > 1
        and incident.shape[1] > v_factors.shape[1] * 2 * PLACES
        and owners & (owners - 1) == 0
    )
    return (paired if fits else gathered_plan)(incident, v_factors, *rest)


def solution(mesh):
    placed = (
        P("rhs", "clus"),
        P("clus", "rhs", None),
        P("clus", "rhs", None),
        P("clus"),
        P("clus"),
        P("clus"),
        P("clus"),
    )
    return jax.shard_map(
        local, mesh=mesh, in_specs=placed, out_specs=P("rhs", "clus"), check_vma=False
    )
```

profile of v0, /device:TPU:0, one launch (start us, length us, event | category | flops | bytes accessed | tf_op | source)
XLA Modules:
  0.0 81.1 jit_solution(17053709264933919727)
XLA Ops:
  0.0 4.1 %collective-permute-start.58 = (bf16[5,256,128]{2,1,0:T(8,128)(2,1)}, bf16[5,256,128]{2,1,0:T(8,128)(2,1)}, u32[]{:S(2)}, u32[]{:S(2)}) collective-permute-start(bf16[5,256,128]{2,1,0:T(8,128)(2,1)} %param.33), channel_id=1, source_target_pairs={{0,16},{4,20},{8,24},{12,28},{16,0},{20,4},{24,8},{28,12},{1,17},{... | collective-permute-start | bytes 983048 | tf_op jit(solution)/shard_map/ppermute | solution.py:206
  4.1 1.6 %collective-permute-start.57 = (bf16[5,256,128]{2,1,0:T(8,128)(2,1)}, bf16[5,256,128]{2,1,0:T(8,128)(2,1)}, u32[]{:S(2)}, u32[]{:S(2)}) collective-permute-start(bf16[5,256,128]{2,1,0:T(8,128)(2,1)} %param.33), channel_id=1, source_target_pairs={{0,8},{4,12},{8,0},{12,4},{16,24},{20,28},{24,16},{28,20},{1,9},{5... | collective-permute-start | bytes 983048 | tf_op jit(solution)/shard_map/ppermute | solution.py:206
  5.8 1.6 %pack.1 = (bf16[104,2048]{1,0:T(8,128)(2,1)S(1)}, bf16[104,2048]{1,0:T(8,128)(2,1)S(1)}) custom-call(s32[2]{0:T(128)S(1)} %pad_add_fusion.3.pos_ref, bf16[104,8192]{1,0:T(8,128)(2,1)} %x_ref.1), custom_call_target="tpu_custom_call" | custom-call | bytes 2555904 | tf_op jit(solution)/shard_map/pack/pallas_call | solution.py:225
  7.4 1.6 %collective-permute-start.55 = (bf16[104,2048]{1,0:T(8,128)(2,1)S(1)}, bf16[104,2048]{1,0:T(8,128)(2,1)S(1)}, u32[]{:S(2)}, u32[]{:S(2)}) collective-permute-start(bf16[104,2048]{1,0:T(8,128)(2,1)S(1)} %get-tuple-element.513), channel_id=1, source_target_pairs={{0,4},{4,0},{8,12},{12,8},{16,20},{20,16},{24,28},{28,24},{1,5},{5... | collective-permute-start | bytes 1277960 | tf_op jit(solution)/shard_map/ppermute | solution.py:209
  9.5 1.6 %collective-permute-start.61 = (s32[5,2]{0,1:T(2,128)S(1)}, s32[5,2]{0,1:T(2,128)S(1)}, u32[]{:S(2)}, u32[]{:S(2)}) collective-permute-start(s32[5,2]{0,1:T(2,128)S(1)} %pad_add_fusion), channel_id=1, source_target_pairs={{0,2},{1,3},{2,0},{3,1},{4,6},{5,7},{6,4},{7,5},{8,10},{9,11},{10,... | collective-permute-start | bytes 128 | tf_op jit(solution)/shard_map/ppermute | solution.py:219
  11.1 2.0 %collective-permute-done.61 = s32[5,2]{0,1:T(2,128)S(1)} collective-permute-done((s32[5,2]{0,1:T(2,128)S(1)}, s32[5,2]{0,1:T(2,128)S(1)}, u32[]{:S(2)}, u32[]{:S(2)}) %collective-permute-start.61) | collective-permute-done | bytes 72 | tf_op jit(solution)/shard_map/ppermute | solution.py:219
  18.0 1.3 %collective-permute-done.58 = bf16[5,256,128]{2,1,0:T(8,128)(2,1)} collective-permute-done((bf16[5,256,128]{2,1,0:T(8,128)(2,1)}, bf16[5,256,128]{2,1,0:T(8,128)(2,1)}, u32[]{:S(2)}, u32[]{:S(2)}) %collective-permute-start.58) | collective-permute-done | bytes 327712 | tf_op jit(solution)/shard_map/ppermute | solution.py:206
  19.3 1.3 %collective-permute-start.60 = (bf16[5,256,128]{2,1,0:T(8,128)(2,1)}, bf16[5,256,128]{2,1,0:T(8,128)(2,1)}, u32[]{:S(2)}, u32[]{:S(2)}) collective-permute-start(bf16[5,256,128]{2,1,0:T(8,128)(2,1)} %collective-permute-done.58), channel_id=1, source_target_pairs={{8,0},{12,4},{16,24},{20,28},{9,1},{13,5},{17,25},{21,29},{10,2},{... | collective-permute-start | bytes 983048 | tf_op jit(solution)/shard_map/ppermute | solution.py:206
  20.6 1.4 %collective-permute-start.59 = (bf16[5,256,128]{2,1,0:T(8,128)(2,1)}, bf16[5,256,128]{2,1,0:T(8,128)(2,1)}, u32[]{:S(2)}, u32[]{:S(2)}) collective-permute-start(bf16[5,256,128]{2,1,0:T(8,128)(2,1)} %param.33), channel_id=1, source_target_pairs={{8,16},{12,20},{16,8},{20,12},{9,17},{13,21},{17,9},{21,13},{10,18... | collective-permute-start | bytes 983048 | tf_op jit(solution)/shard_map/ppermute | solution.py:206
  23.2 4.4 %collective-permute-done.56 = bf16[104,2048]{1,0:T(8,128)(2,1)S(1)} collective-permute-done((bf16[104,2048]{1,0:T(8,128)(2,1)S(1)}, bf16[104,2048]{1,0:T(8,128)(2,1)S(1)}, u32[]{:S(2)}, u32[]{:S(2)}) %collective-permute-start.56) | collective-permute-done | bytes 426016 | tf_op jit(solution)/shard_map/ppermute | solution.py:209
  27.6 2.8 %collective-permute-done.60 = bf16[5,256,128]{2,1,0:T(8,128)(2,1)} collective-permute-done((bf16[5,256,128]{2,1,0:T(8,128)(2,1)}, bf16[5,256,128]{2,1,0:T(8,128)(2,1)}, u32[]{:S(2)}, u32[]{:S(2)}) %collective-permute-start.60) | collective-permute-done | bytes 327712 | tf_op jit(solution)/shard_map/ppermute | solution.py:206
  30.3 49.5 %conditional.1 = (bf16[104,8192]{1,0:T(8,128)(2,1)S(1)}) conditional(s32[]{:T(128)} %clamp.3, (s32[5]{0:T(128)S(1)}, s32[2]{0:T(128)S(1)}, s32[5]{0:T(128)S(1)}, bf16[104,8192]{1,0:T(8,128)(2,1)}, bf16[104,2048]{1,0:T(8,128)(2,1)S(1)}, /*index=5*/bf16[104,2048]{1,0:T(8,128)(2,1)S(1)}, bf16[5,256,128]{2,1,0:T(8,128)(2,1)}, ...), branch_computations={%region_5.10_spmd, %region_10.15_spmd, %region_15.20_spmd, %region... | conditional | flops 2455675904 | bytes 55455392 | solution.py:348
  30.4 2.8 %compress.6 = (f32[5,2,112,128]{3,2,1,0:T(8,128)S(1)}, bf16[5,2,112,128]{3,2,1,0:T(8,128)(2,1)S(1)}) custom-call(s32[2]{0:T(128)S(1)} %get-tuple-element.343.pos_ref, s32[5]{0:T(128)S(1)} %get-tuple-element.547.source_ref, bf16[104,8192]{1,0:T(8,128)(2,1)} %get-tuple-element.349.x_ref, bf16[104,2048]{1,0:T(8,128)(2,1)S(1)} %get-tuple-element.350.xl_ref, ...), custom_call_target="tpu_custom_call" | custom-call | flops 272629760 | bytes 3866624 | tf_op jit(solution)/shard_map/cond/branch_1_fun/compress/pallas_call | solution.py:271
  33.2 1.3 %collective-permute-start.35 = (bf16[5,2,112,128]{3,2,1,0:T(8,128)(2,1)S(1)}, bf16[5,2,112,128]{3,2,1,0:T(8,128)(2,1)S(1)}, u32[]{:S(2)}, u32[]{:S(2)}) collective-permute-start(bf16[5,2,112,128]{3,2,1,0:T(8,128)(2,1)S(1)} %get-tuple-element.358), channel_id=1, source_target_pairs={{0,4},{4,0},{8,12},{12,8},{16,20},{20,16},{24,28},{28,24},{1,5},{5... | collective-permute-start | bytes 860168 | tf_op jit(solution)/shard_map/cond/branch_1_fun/ppermute | solution.py:209
  34.5 6.3 %collective-permute-start.37 = (bf16[6,256,128]{2,1,0:T(8,128)(2,1)S(1)}, bf16[6,256,128]{2,1,0:T(8,128)(2,1)S(1)}, u32[]{:S(2)}, u32[]{:S(2)}) collective-permute-start(bf16[6,256,128]{2,1,0:T(8,128)(2,1)S(1)} %slice.13.u_ref), channel_id=1, source_target_pairs={{0,8},{4,12},{8,0},{12,4},{16,24},{20,28},{24,16},{28,20},{1,9},{5... | collective-permute-start | bytes 1179656 | tf_op jit(solution)/shard_map/cond/branch_1_fun/ppermute | solution.py:206
  40.8 1.2 %collective-permute-start.38 = (bf16[6,256,128]{2,1,0:T(8,128)(2,1)S(1)}, bf16[6,256,128]{2,1,0:T(8,128)(2,1)S(1)}, u32[]{:S(2)}, u32[]{:S(2)}) collective-permute-start(bf16[6,256,128]{2,1,0:T(8,128)(2,1)S(1)} %slice.13.u_ref), channel_id=1, source_target_pairs={{0,16},{4,20},{8,24},{12,28},{16,0},{20,4},{24,8},{28,12},{1,17},{... | collective-permute-start | bytes 1179656 | tf_op jit(solution)/shard_map/cond/branch_1_fun/ppermute | solution.py:206
  42.8 6.8 %while.92 = (s32[]{:T(128)}, bf16[5,2,112,128]{3,2,1,0:T(8,128)(2,1)S(1)}, s32[]{:T(128)}, s32[]{:T(128)}) while((s32[]{:T(128)}, bf16[5,2,112,128]{3,2,1,0:T(8,128)(2,1)S(1)}, s32[]{:T(128)}, s32[]{:T(128)}) %tuple.202), condition=%wide.region_12.12_spmd, body=%wide.region_11.11_spmd.sunk | while | flops 2 | bytes 1720413 | solution.py:297
  42.8 1.5 %collective-permute-start.33 = (bf16[5,2,112,128]{3,2,1,0:T(8,128)(2,1)S(1)}, bf16[5,2,112,128]{3,2,1,0:T(8,128)(2,1)S(1)}, u32[]{:S(2)}, u32[]{:S(2)}) collective-permute-start(bf16[5,2,112,128]{3,2,1,0:T(8,128)(2,1)S(1)} %get-tuple-element.917), channel_id=1, source_target_pairs={{0,2},{1,3},{2,0},{3,1},{4,6},{5,7},{6,4},{7,5},{8,10},{9,11},{10,... | collective-permute-start | bytes 860168 | tf_op jit(solution)/shard_map/cond/branch_1_fun/while/body/ppermute | solution.py:219
  44.4 5.2 %collective-permute-done.33 = bf16[5,2,112,128]{3,2,1,0:T(8,128)(2,1)S(1)} collective-permute-done((bf16[5,2,112,128]{3,2,1,0:T(8,128)(2,1)S(1)}, bf16[5,2,112,128]{3,2,1,0:T(8,128)(2,1)S(1)}, u32[]{:S(2)}, u32[]{:S(2)}) %collective-permute-start.33) | collective-permute-done | bytes 286752 | tf_op jit(solution)/shard_map/cond/branch_1_fun/while/body/ppermute | solution.py:219
  49.7 2.1 %while.93 = (s32[]{:T(128)}, bf16[10,2,112,128]{3,2,1,0:T(8,128)(2,1)S(1)}, s32[]{:T(128)}, s32[]{:T(128)}) while((s32[]{:T(128)}, bf16[10,2,112,128]{3,2,1,0:T(8,128)(2,1)S(1)}, s32[]{:T(128)}, s32[]{:T(128)}) %tuple.205), condition=%wide.region_14.14_spmd, body=%wide.region_13.13_spmd.sunk | while | flops 2 | bytes 3440733 | solution.py:297
  49.8 2.0 %collective-permute-done.34 = bf16[10,2,112,128]{3,2,1,0:T(8,128)(2,1)S(1)} collective-permute-done((bf16[10,2,112,128]{3,2,1,0:T(8,128)(2,1)S(1)}, bf16[10,2,112,128]{3,2,1,0:T(8,128)(2,1)S(1)}, u32[]{:S(2)}, u32[]{:S(2)}) %collective-permute-start.34) | collective-permute-done | bytes 573472 | tf_op jit(solution)/shard_map/cond/branch_1_fun/while/body/ppermute | solution.py:219
  52.0 7.9 %collective-permute-done.38.refs_0_ = bf16[6,256,128]{2,1,0:T(8,128)(2,1)S(1)} collective-permute-done((bf16[6,256,128]{2,1,0:T(8,128)(2,1)S(1)}, bf16[6,256,128]{2,1,0:T(8,128)(2,1)S(1)}, u32[]{:S(2)}, u32[]{:S(2)}) %collective-permute-start.38) | collective-permute-done | bytes 393248 | tf_op jit(solution)/shard_map/cond/branch_1_fun/ppermute | solution.py:206
  60.5 1.5 %collective-permute-start.41 = (bf16[6,256,128]{2,1,0:T(8,128)(2,1)S(1)}, bf16[6,256,128]{2,1,0:T(8,128)(2,1)S(1)}, u32[]{:S(2)}, u32[]{:S(2)}) collective-permute-start(bf16[6,256,128]{2,1,0:T(8,128)(2,1)S(1)} %collective-permute-done.38.refs_0_), channel_id=1, source_target_pairs={{8,0},{12,4},{16,24},{20,28},{9,1},{13,5},{17,25},{21,29},{10,2},{... | collective-permute-start | bytes 1179656 | tf_op jit(solution)/shard_map/cond/branch_1_fun/ppermute | solution.py:206
  62.1 1.1 %land.6.rows_ref = bf16[6,4,224,128]{3,2,1,0:T(8,128)(2,1)S(1)} custom-call(s32[10]{0:T(128)S(1)} %select_reduce_fusion.1.index_ref, s32[10]{0:T(128)S(1)} %copy-done.37, s32[10]{0:T(128)S(1)} %copy-done.28, bf16[20,2,112,128]{3,2,1,0:T(8,128)(2,1)S(1)} %pad_maximum_fusion.2.comp_ref), custom_call_target="tpu_custom_call" | custom-call | bytes 5734400 | tf_op jit(solution)/shard_map/cond/branch_1_fun/land/pallas_call | solution.py:303
  63.3 1.2 %expand.18 = (bf16[104,1024]{1,0:T(8,128)(2,1)S(1)}, bf16[104,1024]{1,0:T(8,128)(2,1)S(1)}) custom-call(s32[2]{0:T(128)S(1)} %copy-done.4, bf16[6,4,224,128]{3,2,1,0:T(8,128)(2,1)S(1)} %land.6.rows_ref, bf16[6,256,128]{2,1,0:T(8,128)(2,1)S(1)} %collective-permute-done.37.refs_0_), custom_call_target="tpu_custom_call" | custom-call | flops 327155712 | bytes 2195456 | tf_op jit(solution)/shard_map/cond/branch_1_fun/expand/pallas_call | solution.py:329
  65.1 1.1 %expand.19 = (bf16[104,1024]{1,0:T(8,128)(2,1)S(1)}, bf16[104,1024]{1,0:T(8,128)(2,1)S(1)}) custom-call(s32[2]{0:T(128)S(1)} %copy-done.4, bf16[6,4,224,128]{3,2,1,0:T(8,128)(2,1)S(1)} %land.6.rows_ref, bf16[6,256,128]{2,1,0:T(8,128)(2,1)S(1)} %collective-permute-done.38.refs_0_), custom_call_target="tpu_custom_call" | custom-call | flops 327155712 | bytes 2195456 | tf_op jit(solution)/shard_map/cond/branch_1_fun/expand/pallas_call | solution.py:329
  66.2 1.6 %collective-permute-start.42 = (bf16[104,1024]{1,0:T(8,128)(2,1)S(1)}, bf16[104,1024]{1,0:T(8,128)(2,1)S(1)}, u32[]{:S(2)}, u32[]{:S(2)}) collective-permute-start(bf16[104,1024]{1,0:T(8,128)(2,1)S(1)} %get-tuple-element.373), channel_id=1, source_target_pairs={{0,4},{4,0},{8,12},{12,8},{16,20},{20,16},{24,28},{28,24},{1,5},{5... | collective-permute-start | bytes 638984 | tf_op jit(solution)/shard_map/cond/branch_1_fun/ppermute | solution.py:209
  68.9 1.5 %collective-permute-done.39.refs_3_ = bf16[104,1024]{1,0:T(8,128)(2,1)S(1)} collective-permute-done((bf16[104,1024]{1,0:T(8,128)(2,1)S(1)}, bf16[104,1024]{1,0:T(8,128)(2,1)S(1)}, u32[]{:S(2)}, u32[]{:S(2)}) %collective-permute-start.39) | collective-permute-done | bytes 213024 | tf_op jit(solution)/shard_map/cond/branch_1_fun/ppermute | solution.py:209
  70.4 1.2 %collective-permute-done.41.refs_1_ = bf16[6,256,128]{2,1,0:T(8,128)(2,1)S(1)} collective-permute-done((bf16[6,256,128]{2,1,0:T(8,128)(2,1)S(1)}, bf16[6,256,128]{2,1,0:T(8,128)(2,1)S(1)}, u32[]{:S(2)}, u32[]{:S(2)}) %collective-permute-start.41) | collective-permute-done | bytes 393248 | tf_op jit(solution)/shard_map/cond/branch_1_fun/ppermute | solution.py:206
  71.5 1.2 %expand.20 = (bf16[104,1024]{1,0:T(8,128)(2,1)S(1)}, bf16[104,1024]{1,0:T(8,128)(2,1)S(1)}) custom-call(s32[2]{0:T(128)S(1)} %copy-done.4, bf16[6,4,224,128]{3,2,1,0:T(8,128)(2,1)S(1)} %land.6.rows_ref, bf16[6,256,128]{2,1,0:T(8,128)(2,1)S(1)} %collective-permute-done.40.refs_0_, bf16[6,256,128]{2,1,0:T(8,128)(2,1)S(1)} %collective-permute-done.41.refs_1_), custom_call_target="tpu_custom_call" | custom-call | flops 327155712 | bytes 2195456 | tf_op jit(solution)/shard_map/cond/branch_1_fun/expand/pallas_call | solution.py:329
  73.3 5.3 %collective-permute-done.43.refs_5_ = bf16[104,1024]{1,0:T(8,128)(2,1)S(1)} collective-permute-done((bf16[104,1024]{1,0:T(8,128)(2,1)S(1)}, bf16[104,1024]{1,0:T(8,128)(2,1)S(1)}, u32[]{:S(2)}, u32[]{:S(2)}) %collective-permute-start.43) | collective-permute-done | bytes 213024 | tf_op jit(solution)/shard_map/cond/branch_1_fun/ppermute | solution.py:209
  79.9 1.2 %copy-done.2 = bf16[104,8192]{1,0:T(8,128)(2,1)} copy-done((bf16[104,8192]{1,0:T(8,128)(2,1)}, bf16[104,8192]{1,0:T(8,128)(2,1)S(1)}, u32[]{:S(2)}) %copy-start.2) | copy-done | bytes 1703960
  (68 shorter events, 9.1 us)
Async XLA Ops:
  0.0 9.5 %copy-start.41 = (s32[5]{0:T(128)S(1)}, s32[5]{0:T(128)}, u32[]{:S(2)}) copy-start(s32[5]{0:T(128)} %param.37) | copy-start | bytes 64
  0.0 9.5 %copy-start.42 = (s32[5]{0:T(128)S(1)}, s32[5]{0:T(128)}, u32[]{:S(2)}) copy-start(s32[5]{0:T(128)} %param.36) | copy-start | bytes 64
  0.0 22.1 %copy-start = (bf16[10,256,128]{2,1,0:T(8,128)(2,1)S(1)}, bf16[10,256,128]{2,1,0:T(8,128)(2,1)}, u32[]{:S(2)}) copy-start(bf16[10,256,128]{2,1,0:T(8,128)(2,1)} %u_ref.1) | copy-start | bytes 1966084
  0.0 19.3 %collective-permute-start.58 = (bf16[5,256,128]{2,1,0:T(8,128)(2,1)}, bf16[5,256,128]{2,1,0:T(8,128)(2,1)}, u32[]{:S(2)}, u32[]{:S(2)}) collective-permute-start(bf16[5,256,128]{2,1,0:T(8,128)(2,1)} %param.33), channel_id=1, source_target_pairs={{0,16},{4,20},{8,24},{12,28},{16,0},{20,4},{24,8},{28,12},{1,17},{... | collective-permute-start | bytes 983048 | tf_op jit(solution)/shard_map/ppermute | solution.py:206
  4.1 19.1 %collective-permute-start.57 = (bf16[5,256,128]{2,1,0:T(8,128)(2,1)}, bf16[5,256,128]{2,1,0:T(8,128)(2,1)}, u32[]{:S(2)}, u32[]{:S(2)}) collective-permute-start(bf16[5,256,128]{2,1,0:T(8,128)(2,1)} %param.33), channel_id=1, source_target_pairs={{0,8},{4,12},{8,0},{12,4},{16,24},{20,28},{24,16},{28,20},{1,9},{5... | collective-permute-start | bytes 983048 | tf_op jit(solution)/shard_map/ppermute | solution.py:206
  5.8 24.6 %copy-start.35 = (s32[5]{0:T(128)S(1)}, s32[5]{0:T(128)}, u32[]{:S(2)}) copy-start(s32[5]{0:T(128)} %param.35) | copy-start | bytes 64
  7.4 15.8 %collective-permute-start.55 = (bf16[104,2048]{1,0:T(8,128)(2,1)S(1)}, bf16[104,2048]{1,0:T(8,128)(2,1)S(1)}, u32[]{:S(2)}, u32[]{:S(2)}) collective-permute-start(bf16[104,2048]{1,0:T(8,128)(2,1)S(1)} %get-tuple-element.513), channel_id=1, source_target_pairs={{0,4},{4,0},{8,12},{12,8},{16,20},{20,16},{24,28},{28,24},{1,5},{5... | collective-permute-start | bytes 1277960 | tf_op jit(solution)/shard_map/ppermute | solution.py:209
  8.9 18.6 %collective-permute-start.56 = (bf16[104,2048]{1,0:T(8,128)(2,1)S(1)}, bf16[104,2048]{1,0:T(8,128)(2,1)S(1)}, u32[]{:S(2)}, u32[]{:S(2)}) collective-permute-start(bf16[104,2048]{1,0:T(8,128)(2,1)S(1)} %get-tuple-element.514), channel_id=1, source_target_pairs={{0,4},{4,0},{8,12},{12,8},{16,20},{20,16},{24,28},{28,24},{1,5},{5... | collective-permute-start | bytes 1277960 | tf_op jit(solution)/shard_map/ppermute | solution.py:209
  9.5 3.6 %collective-permute-start.61 = (s32[5,2]{0,1:T(2,128)S(1)}, s32[5,2]{0,1:T(2,128)S(1)}, u32[]{:S(2)}, u32[]{:S(2)}) collective-permute-start(s32[5,2]{0,1:T(2,128)S(1)} %pad_add_fusion), channel_id=1, source_target_pairs={{0,2},{1,3},{2,0},{3,1},{4,6},{5,7},{6,4},{7,5},{8,10},{9,11},{10,... | collective-permute-start | bytes 128 | tf_op jit(solution)/shard_map/ppermute | solution.py:219
  13.2 1.1 %collective-permute-start.62 = (s32[10,2]{0,1:T(2,128)S(1)}, s32[10,2]{0,1:T(2,128)S(1)}, u32[]{:S(2)}, u32[]{:S(2)}) collective-permute-start(s32[10,2]{0,1:T(2,128)S(1)} %pad_add_fusion.1), channel_id=1, source_target_pairs={{0,1},{1,0},{2,3},{3,2},{4,5},{5,4},{6,7},{7,6},{8,9},{9,8},{10,11... | collective-permute-start | bytes 248 | tf_op jit(solution)/shard_map/ppermute | solution.py:219
  19.3 11.0 %collective-permute-start.60 = (bf16[5,256,128]{2,1,0:T(8,128)(2,1)}, bf16[5,256,128]{2,1,0:T(8,128)(2,1)}, u32[]{:S(2)}, u32[]{:S(2)}) collective-permute-start(bf16[5,256,128]{2,1,0:T(8,128)(2,1)} %collective-permute-done.58), channel_id=1, source_target_pairs={{8,0},{12,4},{16,24},{20,28},{9,1},{13,5},{17,25},{21,29},{10,2},{... | collective-permute-start | bytes 983048 | tf_op jit(solution)/shard_map/ppermute | solution.py:206
  20.6 9.8 %collective-permute-start.59 = (bf16[5,256,128]{2,1,0:T(8,128)(2,1)}, bf16[5,256,128]{2,1,0:T(8,128)(2,1)}, u32[]{:S(2)}, u32[]{:S(2)}) collective-permute-start(bf16[5,256,128]{2,1,0:T(8,128)(2,1)} %param.33), channel_id=1, source_target_pairs={{8,16},{12,20},{16,8},{20,12},{9,17},{13,21},{17,9},{21,13},{10,18... | collective-permute-start | bytes 983048 | tf_op jit(solution)/shard_map/ppermute | solution.py:206
  30.3 2.8 %copy-start.3 = (s32[2]{0:T(128)}, s32[2]{0:T(128)S(1)}, u32[]{:S(2)}) copy-start(s32[2]{0:T(128)S(1)} %get-tuple-element.343.pos_ref) | copy-start | bytes 28 | tf_op jit(solution)/shard_map/cond
  30.4 2.8 %copy-start.11 = (s32[10,20]{1,0:T(8,128)}, s32[10,20]{1,0:T(8,128)S(1)}, u32[]{:S(2)}) copy-start(s32[10,20]{1,0:T(8,128)S(1)} %get-tuple-element.555) | copy-start | bytes 2404 | tf_op jit(solution)/shard_map/cond
  30.4 2.8 %copy-start.19 = (pred[10,20]{1,0:T(8,128)(4,1)}, pred[10,20]{1,0:T(8,128)(4,1)S(1)}, u32[]{:S(2)}) copy-start(pred[10,20]{1,0:T(8,128)(4,1)S(1)} %get-tuple-element.554) | copy-start | bytes 604 | tf_op jit(solution)/shard_map/cond
  30.4 2.8 %copy-start.27 = (s32[10]{0:T(128)}, s32[10]{0:T(128)S(1)}, u32[]{:S(2)}) copy-start(s32[10]{0:T(128)S(1)} %get-tuple-element.346.offset_ref) | copy-start | bytes 124 | tf_op jit(solution)/shard_map/cond
  33.2 8.9 %collective-permute-start.35 = (bf16[5,2,112,128]{3,2,1,0:T(8,128)(2,1)S(1)}, bf16[5,2,112,128]{3,2,1,0:T(8,128)(2,1)S(1)}, u32[]{:S(2)}, u32[]{:S(2)}) collective-permute-start(bf16[5,2,112,128]{3,2,1,0:T(8,128)(2,1)S(1)} %get-tuple-element.358), channel_id=1, source_target_pairs={{0,4},{4,0},{8,12},{12,8},{16,20},{20,16},{24,28},{28,24},{1,5},{5... | collective-permute-start | bytes 860168 | tf_op jit(solution)/shard_map/cond/branch_1_fun/ppermute | solution.py:209
  34.5 28.8 %collective-permute-start.37 = (bf16[6,256,128]{2,1,0:T(8,128)(2,1)S(1)}, bf16[6,256,128]{2,1,0:T(8,128)(2,1)S(1)}, u32[]{:S(2)}, u32[]{:S(2)}) collective-permute-start(bf16[6,256,128]{2,1,0:T(8,128)(2,1)S(1)} %slice.13.u_ref), channel_id=1, source_target_pairs={{0,8},{4,12},{8,0},{12,4},{16,24},{20,28},{24,16},{28,20},{1,9},{5... | collective-permute-start | bytes 1179656 | tf_op jit(solution)/shard_map/cond/branch_1_fun/ppermute | solution.py:206
  40.8 19.0 %collective-permute-start.38 = (bf16[6,256,128]{2,1,0:T(8,128)(2,1)S(1)}, bf16[6,256,128]{2,1,0:T(8,128)(2,1)S(1)}, u32[]{:S(2)}, u32[]{:S(2)}) collective-permute-start(bf16[6,256,128]{2,1,0:T(8,128)(2,1)S(1)} %slice.13.u_ref), channel_id=1, source_target_pairs={{0,16},{4,20},{8,24},{12,28},{16,0},{20,4},{24,8},{28,12},{1,17},{... | collective-permute-start | bytes 1179656 | tf_op jit(solution)/shard_map/cond/branch_1_fun/ppermute | solution.py:206
  42.2 25.6 %collective-permute-start.36 = (bf16[6,256,128]{2,1,0:T(8,128)(2,1)S(1)}, bf16[6,256,128]{2,1,0:T(8,128)(2,1)S(1)}, u32[]{:S(2)}, u32[]{:S(2)}) collective-permute-start(bf16[6,256,128]{2,1,0:T(8,128)(2,1)S(1)} %slice.13.u_ref), channel_id=1, source_target_pairs={{0,4},{4,0},{8,12},{12,8},{16,20},{20,16},{24,28},{28,24},{1,5},{5... | collective-permute-start | bytes 1179656 | tf_op jit(solution)/shard_map/cond/branch_1_fun/ppermute | solution.py:209
  42.8 6.7 %collective-permute-start.33 = (bf16[5,2,112,128]{3,2,1,0:T(8,128)(2,1)S(1)}, bf16[5,2,112,128]{3,2,1,0:T(8,128)(2,1)S(1)}, u32[]{:S(2)}, u32[]{:S(2)}) collective-permute-start(bf16[5,2,112,128]{3,2,1,0:T(8,128)(2,1)S(1)} %get-tuple-element.917), channel_id=1, source_target_pairs={{0,2},{1,3},{2,0},{3,1},{4,6},{5,7},{6,4},{7,5},{8,10},{9,11},{10,... | collective-permute-start | bytes 860168 | tf_op jit(solution)/shard_map/cond/branch_1_fun/while/body/ppermute | solution.py:219
  49.7 2.0 %collective-permute-start.34 = (bf16[10,2,112,128]{3,2,1,0:T(8,128)(2,1)S(1)}, bf16[10,2,112,128]{3,2,1,0:T(8,128)(2,1)S(1)}, u32[]{:S(2)}, u32[]{:S(2)}) collective-permute-start(bf16[10,2,112,128]{3,2,1,0:T(8,128)(2,1)S(1)} %get-tuple-element.929), channel_id=1, source_target_pairs={{0,1},{1,0},{2,3},{3,2},{4,5},{5,4},{6,7},{7,6},{8,9},{9,8},{10,11... | collective-permute-start | bytes 1720328 | tf_op jit(solution)/shard_map/cond/branch_1_fun/while/body/ppermute | solution.py:219
  51.8 10.2 %copy-start.12 = (s32[10,20]{1,0:T(8,128)S(1)}, s32[10,20]{1,0:T(8,128)}, u32[]{:S(2)}) copy-start(s32[10,20]{1,0:T(8,128)} %copy-done.11) | copy-start | bytes 2404 | tf_op jit(solution)/shard_map/cond
  51.8 10.2 %copy-start.20 = (pred[10,20]{1,0:T(8,128)(4,1)S(1)}, pred[10,20]{1,0:T(8,128)(4,1)}, u32[]{:S(2)}) copy-start(pred[10,20]{1,0:T(8,128)(4,1)} %copy-done.19) | copy-start | bytes 604 | tf_op jit(solution)/shard_map/cond
  51.8 10.3 %copy-start.28 = (s32[10]{0:T(128)S(1)}, s32[10]{0:T(128)}, u32[]{:S(2)}) copy-start(s32[10]{0:T(128)} %copy-done.27) | copy-start | bytes 124 | tf_op jit(solution)/shard_map/cond
  51.8 10.3 %copy-start.37 = (s32[10]{0:T(128)S(1)}, s32[10]{0:T(128)}, u32[]{:S(2)}) copy-start(s32[10]{0:T(128)} %get-tuple-element.567.target_ref) | copy-start | bytes 124 | tf_op jit(solution)/shard_map/cond
  59.8 10.6 %collective-permute-start.40 = (bf16[6,256,128]{2,1,0:T(8,128)(2,1)S(1)}, bf16[6,256,128]{2,1,0:T(8,128)(2,1)S(1)}, u32[]{:S(2)}, u32[]{:S(2)}) collective-permute-start(bf16[6,256,128]{2,1,0:T(8,128)(2,1)S(1)} %slice.13.u_ref), channel_id=1, source_target_pairs={{8,16},{12,20},{16,8},{20,12},{9,17},{13,21},{17,9},{21,13},{10,18... | collective-permute-start | bytes 1179656 | tf_op jit(solution)/shard_map/cond/branch_1_fun/ppermute | solution.py:206
  60.5 11.1 %collective-permute-start.41 = (bf16[6,256,128]{2,1,0:T(8,128)(2,1)S(1)}, bf16[6,256,128]{2,1,0:T(8,128)(2,1)S(1)}, u32[]{:S(2)}, u32[]{:S(2)}) collective-permute-start(bf16[6,256,128]{2,1,0:T(8,128)(2,1)S(1)} %collective-permute-done.38.refs_0_), channel_id=1, source_target_pairs={{8,0},{12,4},{16,24},{20,28},{9,1},{13,5},{17,25},{21,29},{10,2},{... | collective-permute-start | bytes 1179656 | tf_op jit(solution)/shard_map/cond/branch_1_fun/ppermute | solution.py:206
  64.5 5.9 %collective-permute-start.39 = (bf16[104,1024]{1,0:T(8,128)(2,1)S(1)}, bf16[104,1024]{1,0:T(8,128)(2,1)S(1)}, u32[]{:S(2)}, u32[]{:S(2)}) collective-permute-start(bf16[104,1024]{1,0:T(8,128)(2,1)S(1)} %get-tuple-element.368), channel_id=1, source_target_pairs={{0,4},{4,0},{8,12},{12,8},{16,20},{20,16},{24,28},{28,24},{1,5},{5... | collective-permute-start | bytes 638984 | tf_op jit(solution)/shard_map/cond/branch_1_fun/ppermute | solution.py:209
  66.2 7.1 %collective-permute-start.42 = (bf16[104,1024]{1,0:T(8,128)(2,1)S(1)}, bf16[104,1024]{1,0:T(8,128)(2,1)S(1)}, u32[]{:S(2)}, u32[]{:S(2)}) collective-permute-start(bf16[104,1024]{1,0:T(8,128)(2,1)S(1)} %get-tuple-element.373), channel_id=1, source_target_pairs={{0,4},{4,0},{8,12},{12,8},{16,20},{20,16},{24,28},{28,24},{1,5},{5... | collective-permute-start | bytes 638984 | tf_op jit(solution)/shard_map/cond/branch_1_fun/ppermute | solution.py:209
  72.7 5.9 %collective-permute-start.43 = (bf16[104,1024]{1,0:T(8,128)(2,1)S(1)}, bf16[104,1024]{1,0:T(8,128)(2,1)S(1)}, u32[]{:S(2)}, u32[]{:S(2)}) collective-permute-start(bf16[104,1024]{1,0:T(8,128)(2,1)S(1)} %get-tuple-element.374), channel_id=1, source_target_pairs={{0,4},{4,0},{8,12},{12,8},{16,20},{20,16},{24,28},{28,24},{1,5},{5... | collective-permute-start | bytes 638984 | tf_op jit(solution)/shard_map/cond/branch_1_fun/ppermute | solution.py:209
  79.9 1.2 %copy-start.2 = (bf16[104,8192]{1,0:T(8,128)(2,1)}, bf16[104,8192]{1,0:T(8,128)(2,1)S(1)}, u32[]{:S(2)}) copy-start(bf16[104,8192]{1,0:T(8,128)(2,1)S(1)} %get-tuple-element.1074) | copy-start | bytes 5111812
  (1 other events, 1.2 us)
where the time goes:
time: 81.8 us; the launch traced here: 81.1 us
  waiting for transfers between devices  34.5 us (42%)
  starting transfers between devices  27.9 us (34%)
  Pallas kernels  11.8 us (14%)
  between operations  2.68 us (3%)
  other arithmetic  1.87 us (2%)
  local copies, waits for them, and re-layouts  1.35 us (2%)
  loops' own time  0.85 us (1%)
    ppermute x8, starting transfers between devices, move(): lax.ppermute(array, 'rhs', [(2 * a + i, 2 * b + i) for a, b in pairs for...  18 us
    ppermute x8, waiting for transfers between devices, move(): lax.ppermute(array, 'rhs', [(2 * a + i, 2 * b + i) for a, b in pairs for...  13 us
    ppermute x7, waiting for transfers between devices, across(): return lax.ppermute(array, 'rhs', [(p, p ^ 1) for p in range(2 * PLACES)])  11.1 us
    ppermute x4, waiting for transfers between devices, swapped(): return lax.ppermute(array, 'clus', [(p, p ^ stage) for p in range(owners)])  10.4 us
    ppermute x7, starting transfers between devices, across(): return lax.ppermute(array, 'rhs', [(p, p ^ 1) for p in range(2 * PLACES)])  6.76 us
    pallas_call x3, Pallas kernels, rest(): call(functools.partial(expand_body, seg, columns), [chunk, chunk], [SMEM,...  3.46 us
    ppermute x4, starting transfers between devices, swapped(): return lax.ppermute(array, 'clus', [(p, p ^ stage) for p in range(owners)])  3.18 us
    pallas_call x1, Pallas kernels, rest(): call(functools.partial(compress_body, seg), [jax.ShapeDtypeStruct((blocks...  2.78 us
  transfers between devices with their start and end apart: 19, of which 11 were waited for; matrix products, arithmetic and copies ran while one was open for 2% of the time, Pallas kernels for 10%

commit v1 on v0

--- a/solution.py
+++ b/solution.py
@@ -36,7 +36,7 @@
 
 
 def compress_body(seg, pos_ref, source_ref, x_ref, xl_ref, xh_ref, *refs):
-    v0, v1, v2, v3, v4, out_ref, send_ref, xn_ref = refs
+    v0, v1, v2, v3, v4, out_ref, low_ref, high_ref, xn_ref = refs
     half, mine = pos_ref[0], pos_ref[1]
     columns = x_ref.shape[0]
     xn_ref[:, : xl_ref.shape[1]] = xl_ref[...]
@@ -69,7 +69,8 @@
     def _():
         run((v0, v1, v2, v4))
 
-    send_ref[...] = out_ref[...].astype(send_ref.dtype)
+    low_ref[...] = out_ref[:, 0].astype(low_ref.dtype)
+    high_ref[...] = out_ref[:, 1].astype(high_ref.dtype)
 
 
 def place_columns(value, offset, store):
@@ -108,36 +109,37 @@
         place_columns(value, offset_ref[slot], store)
 
 
-def lined_up(ref, rows):
-    return jnp.concatenate([ref[tile].reshape(rows, ref.shape[-1]) for tile in range(ref.shape[0])], axis=1)
-
-
-def expand_body(seg, columns, pos_ref, rows_ref, *refs):
+def lined_up(rows, *refs):
+    tiles = [ref[tile].reshape(rows, ref.shape[-1]) for ref in refs for tile in range(ref.shape[0])]
+    return jnp.concatenate(tiles, axis=1)
+
+
+def expand_body(seg, columns, choices, pos_ref, rows_ref, *refs):
     own_ref, other_ref, acc = refs[-3:]
     half, mine = pos_ref[0], pos_ref[1]
     clusters, sides, padded = acc.shape[:3]
 
-    def run(shard):
+    def run(choice):
         product = lax.dot_general(
-            lined_up(rows_ref, clusters * sides * padded),
-            lined_up(shard, seg),
+            lined_up(clusters * sides * padded, rows_ref),
+            lined_up(seg, *refs[choice]),
             (((1,), (1,)), ((), ())),
             preferred_element_type=jnp.float32,
         )
         acc[...] = product.reshape(acc.shape)
 
-    if len(refs) == 4:
-        run(refs[0])
+    if len(choices) == 1:
+        run(choices[0])
     else:
         inner = (mine == 1) | (mine == 2)
 
         @pl.when(inner)
         def _():
-            run(refs[0])
+            run(choices[0])
 
         @pl.when(jnp.logical_not(inner))
         def _():
-            run(refs[1])
+            run(choices[1])
 
     for target in range(clusters):
         span = slice(target * seg, (target + 1) * seg)
@@ -157,7 +159,7 @@
     for shard, place in ((u_ref, half), (side_ref, 1 - half)):
         product = lax.dot_general(
             rows,
-            lined_up(shard, seg),
+            lined_up(seg, shard),
             (((1,), (1,)), ((), ())),
             preferred_element_type=jnp.float32,
         )
@@ -258,21 +260,24 @@
         scratch=[pltpu.VMEM((capacity + 2, seg, rank_max), jnp.float32)],
     )(offset, used, u_factors)
 
-    x_low, x_high = [across(part) for part in packed]
-    v_ends = move(after(v_far, *packed), ends)
-    v_middle = move(after(v_factors, v_far), middle)
     arrived = lax.optimization_barrier(
-        (x_low, x_high, v_near, v_far, v_middle, v_ends, squeezed, level)
-    )
-
-    def rest(count, x_low, x_high, v_near, v_far, v_middle, v_ends, squeezed):
+        (across(packed[0]), packed[1], v_near, v_far, squeezed, level)
+    )
+
+    def rest(count, x_low, high, v_near, v_far, squeezed):
+        v_ends, v_middle = move(v_far, ends), move(v_factors, middle)
+        x_high = across(high)
         target_factors = squeezed[:count]
-        u_far, u_near = move(target_factors, far), move(target_factors, near)
-        partial, sent = call(
+        u_first, u_second = [
+            move(part, far) for part in (target_factors[: count // 2], target_factors[count // 2 :])
+        ]
+        u_near = move(target_factors, near)
+        partial, *sent = call(
             functools.partial(compress_body, seg),
             [
                 jax.ShapeDtypeStruct((blocks, 2, padded, rank_max), jnp.float32),
-                jax.ShapeDtypeStruct((blocks, 2, padded, rank_max), jnp.bfloat16),
+                jax.ShapeDtypeStruct((blocks, padded, rank_max), jnp.bfloat16),
+                jax.ShapeDtypeStruct((blocks, padded, rank_max), jnp.bfloat16),
             ],
             [SMEM, SMEM] + [VMEM] * 8,
             "compress",
@@ -283,7 +288,7 @@
             position, block_source, incident, x_low, x_high,
             v_factors, v_near, v_far, v_middle, v_ends,
         )
-        received = across(sent)
+        received = jnp.stack([across(part) for part in sent], axis=1)
         u_side = across(after(target_factors, received))
         rank_index = lax.broadcasted_iota(jnp.int32, (blocks, 1, 1, rank_max), 3)
         rows = jnp.where(
@@ -292,14 +297,14 @@
             0.0,
         ).astype(jnp.bfloat16)
 
-        rounds, gathered = 1 + jnp.minimum(me, 0), rows
+        rounds, gathered = 1 + jnp.minimum(me, 0), after(rows, u_first)
         for stage in stages:
             other = lax.fori_loop(
                 0, rounds, lambda _, array, stage=stage: swapped(array, stage), gathered
             )
             gathered = jnp.concatenate([gathered, other], axis=0)
-        u_ends = move(after(u_far, gathered), ends)
-        u_middle = move(after(target_factors, u_far, gathered), middle)
+        u_ends = [move(after(part, gathered), ends) for part in (u_first, u_second)]
+        u_middle = move(after(target_factors, u_second, gathered), middle)
         slot_rows = call(
             land_body,
             jax.ShapeDtypeStruct((count, clusters, 2 * padded, rank_max), jnp.bfloat16),
@@ -321,13 +326,17 @@
             scratch=[pltpu.VMEM((clusters, padded, seg), jnp.float32)],
         )(position, slot_rows, target_factors, u_side)
         finished = []
-        for step, shards in ((1, [u_near]), (2, [u_far]), (3, [u_middle, u_ends])):
+        for step, shards, choices in (
+            (1, [u_near], [slice(0, 1)]),
+            (2, [u_first, u_second], [slice(0, 2)]),
+            (3, [u_middle, *u_ends], [slice(0, 1), slice(1, 3)]),
+        ):
             if finished:
                 slot_rows = after(slot_rows, own_parts[finished[-1]])
             if len(finished) == 2:
                 slot_rows = after(slot_rows, first, other_parts[finished[0]])
             own, other = call(
-                functools.partial(expand_body, seg, columns),
+                functools.partial(expand_body, seg, columns, choices),
                 [chunk, chunk],
                 [SMEM, VMEM] + [VMEM] * len(shards),
                 "expand",

time: 81.8 us -> 86.5 us (1.057); the launches traced: 81.1 us -> 86.8 us
  local copies, waits for them, and re-layouts: 1.35 us -> 5.77 us
  waiting for transfers between devices: 34.5 us -> 30.8 us
  Pallas kernels: 11.8 us -> 14.9 us
  starting transfers between devices: 27.9 us -> 29.5 us
    ppermute x7 -> x8, starting transfers between devices: 6.76 us -> 10.5 us  [across(): return lax.ppermute(array, 'rhs', [(p, p ^ 1) for p in range(2 * PLACES)])]
    slice x0 -> x2, local copies, waits for them, and re-layouts: none -> 2.59 us  [the longest x1 1.65 us: rest(): target_factors[count // 2:]]
    ppermute x8 -> x10, starting transfers between devices: 18 us -> 15.7 us  [move(): lax.ppermute(array, 'rhs', [(2 * a + i, 2 * b + i) for a, b in pairs for...]
    ppermute x7 -> x8, waiting for transfers between devices: 11.1 us -> 9 us  [across(): return lax.ppermute(array, 'rhs', [(p, p ^ 1) for p in range(2 * PLACES)])]
    ppermute x8 -> x10, waiting for transfers between devices: 13 us -> 11.3 us  [move(): lax.ppermute(array, 'rhs', [(2 * a + i, 2 * b + i) for a, b in pairs for...]
    pallas_call x1, Pallas kernels: 0.7 us -> 1.9 us  [rest(): call(functools.partial(join_body, seg, clusters), jax.ShapeDtypeStruct((c...]
    unnamed x10, local copies, waits for them, and re-layouts: 1.19 us -> 0.02 us
    concatenate x0 -> x1, local copies, waits for them, and re-layouts: none -> 1.15 us  [rest(): gathered = jnp.concatenate([gathered, other], axis=0)]
  transfers between devices with their start and end apart: 19 -> 22, of which waited for: 11 -> 10; matrix products, arithmetic and copies ran while one was open for 2% -> 10% of each run, Pallas kernels for 10% -> 15%
where the time goes in v1:
time: 86.5 us; the launch traced here: 86.8 us
  waiting for transfers between devices  30.8 us (36%)
  starting transfers between devices  29.5 us (34%)
  Pallas kernels  14.9 us (17%)
  local copies, waits for them, and re-layouts  5.77 us (7%)
  between operations  2.64 us (3%)
  other arithmetic  2.58 us (3%)
    ppermute x10, starting transfers between devices, move(): lax.ppermute(array, 'rhs', [(2 * a + i, 2 * b + i) for a, b in pairs for...  15.7 us
    ppermute x10, waiting for transfers between devices, move(): lax.ppermute(array, 'rhs', [(2 * a + i, 2 * b + i) for a, b in pairs for...  11.3 us
    ppermute x8, starting transfers between devices, across(): return lax.ppermute(array, 'rhs', [(p, p ^ 1) for p in range(2 * PLACES)])  10.5 us
    ppermute x4, waiting for transfers between devices, swapped(): return lax.ppermute(array, 'clus', [(p, p ^ stage) for p in range(owners)])  10.5 us
    ppermute x8, waiting for transfers between devices, across(): return lax.ppermute(array, 'rhs', [(p, p ^ 1) for p in range(2 * PLACES)])  9 us
    pallas_call x3, Pallas kernels, rest(): call(functools.partial(expand_body, seg, columns, choices), [chunk, chunk...  3.82 us
    ppermute x4, starting transfers between devices, swapped(): return lax.ppermute(array, 'clus', [(p, p ^ stage) for p in range(owners)])  3.25 us
    pallas_call x1, Pallas kernels, rest(): call(functools.partial(compress_body, seg), [jax.ShapeDtypeStruct((blocks...  2.58 us
  transfers between devices with their start and end apart: 22, of which 10 were waited for; matrix products, arithmetic and copies ran while one was open for 10% of the time, Pallas kernels for 15%

profile of v1, /device:TPU:0, one launch (start us, length us, event | category | flops | bytes accessed | tf_op | source)
XLA Modules:
  0.0 86.8 jit_solution(4923327296052486089)
XLA Ops:
  0.0 3.1 %collective-permute-start.86 = (bf16[5,256,128]{2,1,0:T(8,128)(2,1)}, bf16[5,256,128]{2,1,0:T(8,128)(2,1)}, u32[]{:S(2)}, u32[]{:S(2)}) collective-permute-start(bf16[5,256,128]{2,1,0:T(8,128)(2,1)} %param.33), channel_id=1, source_target_pairs={{0,8},{4,12},{8,0},{12,4},{16,24},{20,28},{24,16},{28,20},{1,9},{5... | collective-permute-start | bytes 983048 | tf_op jit(solution)/shard_map/ppermute | solution.py:208
  3.1 2.6 %collective-permute-start.87 = (bf16[5,256,128]{2,1,0:T(8,128)(2,1)}, bf16[5,256,128]{2,1,0:T(8,128)(2,1)}, u32[]{:S(2)}, u32[]{:S(2)}) collective-permute-start(bf16[5,256,128]{2,1,0:T(8,128)(2,1)} %param.33), channel_id=1, source_target_pairs={{0,16},{4,20},{8,24},{12,28},{16,0},{20,4},{24,8},{28,12},{1,17},{... | collective-permute-start | bytes 983048 | tf_op jit(solution)/shard_map/ppermute | solution.py:208
  5.8 2.4 %pack.1 = (bf16[104,2048]{1,0:T(8,128)(2,1)S(1)}, bf16[104,2048]{1,0:T(8,128)(2,1)}) custom-call(s32[2]{0:T(128)S(1)} %pad_add_fusion.3.pos_ref, bf16[104,8192]{1,0:T(8,128)(2,1)} %x_ref.1), custom_call_target="tpu_custom_call" | custom-call | bytes 2555904 | tf_op jit(solution)/shard_map/pack/pallas_call | solution.py:227
  8.1 1.5 %collective-permute-start.85 = (bf16[104,2048]{1,0:T(8,128)(2,1)S(1)}, bf16[104,2048]{1,0:T(8,128)(2,1)S(1)}, u32[]{:S(2)}, u32[]{:S(2)}) collective-permute-start(bf16[104,2048]{1,0:T(8,128)(2,1)S(1)} %get-tuple-element.494), channel_id=1, source_target_pairs={{0,4},{4,0},{8,12},{12,8},{16,20},{20,16},{24,28},{28,24},{1,5},{5... | collective-permute-start | bytes 1277960 | tf_op jit(solution)/shard_map/ppermute | solution.py:211
  9.6 1.6 %collective-permute-start.88 = (s32[5,2]{0,1:T(2,128)S(1)}, s32[5,2]{0,1:T(2,128)S(1)}, u32[]{:S(2)}, u32[]{:S(2)}) collective-permute-start(s32[5,2]{0,1:T(2,128)S(1)} %pad_add_fusion), channel_id=1, source_target_pairs={{0,2},{1,3},{2,0},{3,1},{4,6},{5,7},{6,4},{7,5},{8,10},{9,11},{10,... | collective-permute-start | bytes 128 | tf_op jit(solution)/shard_map/ppermute | solution.py:221
  11.2 2.0 %collective-permute-done.88 = s32[5,2]{0,1:T(2,128)S(1)} collective-permute-done((s32[5,2]{0,1:T(2,128)S(1)}, s32[5,2]{0,1:T(2,128)S(1)}, u32[]{:S(2)}, u32[]{:S(2)}) %collective-permute-start.88) | collective-permute-done | bytes 72 | tf_op jit(solution)/shard_map/ppermute | solution.py:221
  18.3 1.9 %squeeze.1 = bf16[10,256,128]{2,1,0:T(8,128)(2,1)} custom-call(s32[10]{0:T(128)S(1)} %select_reduce_fusion.5.offset_ref, s32[10]{0:T(128)S(1)} %select_reduce_fusion.6.used_ref, bf16[10,256,128]{2,1,0:T(8,128)(2,1)S(1)} %copy-done), custom_call_target="tpu_custom_call" | custom-call | bytes 1310720 | tf_op jit(solution)/shard_map/squeeze/pallas_call | solution.py:254
  20.6 66.2 %conditional.1 = (bf16[104,8192]{1,0:T(8,128)(2,1)}) conditional(s32[]{:T(128)} %clamp.3, (s32[5]{0:T(128)S(1)}, bf16[104,2048]{1,0:T(8,128)(2,1)}, bf16[5,256,128]{2,1,0:T(8,128)(2,1)}, bf16[5,256,128]{2,1,0:T(8,128)(2,1)}, s32[2]{0:T(128)S(1)}, /*index=5*/s32[5]{0:T(128)S(1)}, bf16[104,8192]{1,0:T(8,128)(2,1)}, ...), branch_computations={%region_5.10_spmd, %region_10.15_spmd, %region_15.20_spmd, %region... | conditional | flops 2454672384 | bytes 63582204 | solution.py:357
  20.9 1.6 %collective-permute-start.36 = (bf16[104,2048]{1,0:T(8,128)(2,1)}, bf16[104,2048]{1,0:T(8,128)(2,1)S(1)}, u32[]{:S(2)}, u32[]{:S(2)}) collective-permute-start(bf16[104,2048]{1,0:T(8,128)(2,1)} %get-tuple-element.375), channel_id=1, source_target_pairs={{0,4},{4,0},{8,12},{12,8},{16,20},{20,16},{24,28},{28,24},{1,5},{5... | collective-permute-start | bytes 1277960 | tf_op jit(solution)/shard_map/cond/branch_2_fun/ppermute | solution.py:211
  23.1 1.3 %collective-permute-start.38 = (bf16[5,256,128]{2,1,0:T(8,128)(2,1)}, bf16[5,256,128]{2,1,0:T(8,128)(2,1)S(1)}, u32[]{:S(2)}, u32[]{:S(2)}) collective-permute-start(bf16[5,256,128]{2,1,0:T(8,128)(2,1)} %get-tuple-element.378.refs_2_), channel_id=1, source_target_pairs={{8,0},{12,4},{16,24},{20,28},{9,1},{13,5},{17,25},{21,29},{10,2},{... | collective-permute-start | bytes 983048 | tf_op jit(solution)/shard_map/cond/branch_2_fun/ppermute | solution.py:208
  25.5 2.7 %collective-permute-start.43 = (bf16[7,256,128]{2,1,0:T(8,128)(2,1)S(1)}, bf16[7,256,128]{2,1,0:T(8,128)(2,1)S(1)}, u32[]{:S(2)}, u32[]{:S(2)}) collective-permute-start(bf16[7,256,128]{2,1,0:T(8,128)(2,1)S(1)} %slice.47.u_ref), channel_id=1, source_target_pairs={{0,8},{4,12},{8,0},{12,4},{16,24},{20,28},{24,16},{28,20},{1,9},{5... | collective-permute-start | bytes 1376264 | tf_op jit(solution)/shard_map/cond/branch_2_fun/ppermute | solution.py:208
  29.1 1.7 %slice.48 = bf16[4,256,128]{2,1,0:T(8,128)(2,1)} slice(bf16[10,256,128]{2,1,0:T(8,128)(2,1)} %get-tuple-element.382), slice={[3:7], [0:256], [0:128]} | slice | bytes 524288 | tf_op jit(solution)/shard_map/cond/branch_2_fun/slice | solution.py:272
  31.8 8.4 %collective-permute-done.38.refs_4_ = bf16[5,256,128]{2,1,0:T(8,128)(2,1)S(1)} collective-permute-done((bf16[5,256,128]{2,1,0:T(8,128)(2,1)}, bf16[5,256,128]{2,1,0:T(8,128)(2,1)S(1)}, u32[]{:S(2)}, u32[]{:S(2)}) %collective-permute-start.38) | collective-permute-done | bytes 327712 | tf_op jit(solution)/shard_map/cond/branch_2_fun/ppermute | solution.py:208
  40.2 2.6 %compress.7 = (f32[5,2,112,128]{3,2,1,0:T(8,128)S(1)}, bf16[5,112,128]{2,1,0:T(8,128)(2,1)S(1)}, bf16[5,112,128]{2,1,0:T(8,128)(2,1)S(1)}) custom-call(s32[2]{0:T(128)S(1)} %get-tuple-element.367.pos_ref, s32[5]{0:T(128)S(1)} %get-tuple-element.525.source_ref, bf16[104,8192]{1,0:T(8,128)(2,1)} %get-tuple-element.373.x_ref, ...), custom_call_target="tpu_custom_call" | custom-call | flops 272629760 | bytes 3866624 | tf_op jit(solution)/shard_map/cond/branch_2_fun/compress/pallas_call | solution.py:275
  43.3 1.6 %collective-permute-start.40 = (bf16[5,112,128]{2,1,0:T(8,128)(2,1)S(1)}, bf16[5,112,128]{2,1,0:T(8,128)(2,1)S(1)}, u32[]{:S(2)}, u32[]{:S(2)}) collective-permute-start(bf16[5,112,128]{2,1,0:T(8,128)(2,1)S(1)} %get-tuple-element.381), channel_id=1, source_target_pairs={{0,4},{4,0},{8,12},{12,8},{16,20},{20,16},{24,28},{28,24},{1,5},{5... | collective-permute-start | bytes 430088 | tf_op jit(solution)/shard_map/cond/branch_2_fun/ppermute | solution.py:211
  46.1 1.9 %collective-permute-done.39 = bf16[5,112,128]{2,1,0:T(8,128)(2,1)S(1)} collective-permute-done((bf16[5,112,128]{2,1,0:T(8,128)(2,1)S(1)}, bf16[5,112,128]{2,1,0:T(8,128)(2,1)S(1)}, u32[]{:S(2)}, u32[]{:S(2)}) %collective-permute-start.39) | collective-permute-done | bytes 143392 | tf_op jit(solution)/shard_map/cond/branch_2_fun/ppermute | solution.py:211
  48.0 1.7 %collective-permute-start.42 = (bf16[7,256,128]{2,1,0:T(8,128)(2,1)S(1)}, bf16[7,256,128]{2,1,0:T(8,128)(2,1)S(1)}, u32[]{:S(2)}, u32[]{:S(2)}) collective-permute-start(bf16[7,256,128]{2,1,0:T(8,128)(2,1)S(1)} %slice.47.u_ref), channel_id=1, source_target_pairs={{0,4},{4,0},{8,12},{12,8},{16,20},{20,16},{24,28},{28,24},{1,5},{5... | collective-permute-start | bytes 1376264 | tf_op jit(solution)/shard_map/cond/branch_2_fun/ppermute | solution.py:211
  49.8 6.7 %while.92 = (s32[]{:T(128)}, bf16[5,2,112,128]{3,2,1,0:T(8,128)(2,1)S(1)}, s32[]{:T(128)}, s32[]{:T(128)}) while((s32[]{:T(128)}, bf16[5,2,112,128]{3,2,1,0:T(8,128)(2,1)S(1)}, s32[]{:T(128)}, s32[]{:T(128)}) %tuple.210), condition=%wide.region_17.17_spmd, body=%wide.region_16.16_spmd.sunk | while | flops 2 | bytes 1720413 | solution.py:302
  49.8 1.6 %collective-permute-start.34 = (bf16[5,2,112,128]{3,2,1,0:T(8,128)(2,1)S(1)}, bf16[5,2,112,128]{3,2,1,0:T(8,128)(2,1)S(1)}, u32[]{:S(2)}, u32[]{:S(2)}) collective-permute-start(bf16[5,2,112,128]{3,2,1,0:T(8,128)(2,1)S(1)} %get-tuple-element.876), channel_id=1, source_target_pairs={{0,2},{1,3},{2,0},{3,1},{4,6},{5,7},{6,4},{7,5},{8,10},{9,11},{10,... | collective-permute-start | bytes 860168 | tf_op jit(solution)/shard_map/cond/branch_2_fun/while/body/ppermute | solution.py:221
  51.4 5.1 %collective-permute-done.34 = bf16[5,2,112,128]{3,2,1,0:T(8,128)(2,1)S(1)} collective-permute-done((bf16[5,2,112,128]{3,2,1,0:T(8,128)(2,1)S(1)}, bf16[5,2,112,128]{3,2,1,0:T(8,128)(2,1)S(1)}, u32[]{:S(2)}, u32[]{:S(2)}) %collective-permute-start.34) | collective-permute-done | bytes 286752 | tf_op jit(solution)/shard_map/cond/branch_2_fun/while/body/ppermute | solution.py:221
  57.5 3.1 %while.93 = (s32[]{:T(128)}, bf16[10,2,112,128]{3,2,1,0:T(8,128)(2,1)}, s32[]{:T(128)}, s32[]{:T(128)}) while((s32[]{:T(128)}, bf16[10,2,112,128]{3,2,1,0:T(8,128)(2,1)}, s32[]{:T(128)}, s32[]{:T(128)}) %tuple.213), condition=%wide.region_19.19_spmd, body=%wide.region_18.18_spmd.sunk | while | flops 2 | bytes 3440733 | solution.py:302
  57.6 2.2 %collective-permute-done.35 = bf16[10,2,112,128]{3,2,1,0:T(8,128)(2,1)S(1)} collective-permute-done((bf16[10,2,112,128]{3,2,1,0:T(8,128)(2,1)}, bf16[10,2,112,128]{3,2,1,0:T(8,128)(2,1)S(1)}, u32[]{:S(2)}, u32[]{:S(2)}) %collective-permute-start.35) | collective-permute-done | bytes 573472 | tf_op jit(solution)/shard_map/cond/branch_2_fun/while/body/ppermute | solution.py:221
  62.5 1.3 %collective-permute-start.48 = (bf16[4,256,128]{2,1,0:T(8,128)(2,1)S(1)}, bf16[4,256,128]{2,1,0:T(8,128)(2,1)S(1)}, u32[]{:S(2)}, u32[]{:S(2)}) collective-permute-start(bf16[4,256,128]{2,1,0:T(8,128)(2,1)S(1)} %collective-permute-done.44.refs_1_), channel_id=1, source_target_pairs={{8,0},{12,4},{16,24},{20,28},{9,1},{13,5},{17,25},{21,29},{10,2},{... | collective-permute-start | bytes 786440 | tf_op jit(solution)/shard_map/cond/branch_2_fun/ppermute | solution.py:208
  65.1 1.3 %expand.21 = (bf16[104,1024]{1,0:T(8,128)(2,1)S(1)}, bf16[104,1024]{1,0:T(8,128)(2,1)S(1)}) custom-call(s32[2]{0:T(128)S(1)} %copy-done.6, bf16[7,4,224,128]{3,2,1,0:T(8,128)(2,1)S(1)} %land.7.rows_ref, bf16[7,256,128]{2,1,0:T(8,128)(2,1)S(1)} %collective-permute-done.43.refs_0_), custom_call_target="tpu_custom_call" | custom-call | flops 381681664 | bytes 2490368 | tf_op jit(solution)/shard_map/cond/branch_2_fun/expand/pallas_call | solution.py:338
  66.4 1.6 %collective-permute-start.45 = (bf16[104,1024]{1,0:T(8,128)(2,1)S(1)}, bf16[104,1024]{1,0:T(8,128)(2,1)S(1)}, u32[]{:S(2)}, u32[]{:S(2)}) collective-permute-start(bf16[104,1024]{1,0:T(8,128)(2,1)S(1)} %get-tuple-element.392), channel_id=1, source_target_pairs={{0,4},{4,0},{8,12},{12,8},{16,20},{20,16},{24,28},{28,24},{1,5},{5... | collective-permute-start | bytes 638984 | tf_op jit(solution)/shard_map/cond/branch_2_fun/ppermute | solution.py:211
  68.0 1.3 %collective-permute-start.47 = (bf16[3,256,128]{2,1,0:T(8,128)(2,1)S(1)}, bf16[3,256,128]{2,1,0:T(8,128)(2,1)S(1)}, u32[]{:S(2)}, u32[]{:S(2)}) collective-permute-start(bf16[3,256,128]{2,1,0:T(8,128)(2,1)S(1)} %collective-permute-done.41.refs_0_), channel_id=1, source_target_pairs={{8,0},{12,4},{16,24},{20,28},{9,1},{13,5},{17,25},{21,29},{10,2},{... | collective-permute-start | bytes 589832 | tf_op jit(solution)/shard_map/cond/branch_2_fun/ppermute | solution.py:208
  72.4 2.0 %collective-permute-done.45.refs_3_ = bf16[104,1024]{1,0:T(8,128)(2,1)S(1)} collective-permute-done((bf16[104,1024]{1,0:T(8,128)(2,1)S(1)}, bf16[104,1024]{1,0:T(8,128)(2,1)S(1)}, u32[]{:S(2)}, u32[]{:S(2)}) %collective-permute-start.45) | collective-permute-done | bytes 213024 | tf_op jit(solution)/shard_map/cond/branch_2_fun/ppermute | solution.py:211
  74.4 2.6 %collective-permute-done.47.refs_1_ = bf16[3,256,128]{2,1,0:T(8,128)(2,1)S(1)} collective-permute-done((bf16[3,256,128]{2,1,0:T(8,128)(2,1)S(1)}, bf16[3,256,128]{2,1,0:T(8,128)(2,1)S(1)}, u32[]{:S(2)}, u32[]{:S(2)}) %collective-permute-start.47) | collective-permute-done | bytes 196640 | tf_op jit(solution)/shard_map/cond/branch_2_fun/ppermute | solution.py:208
  77.0 1.3 %expand.23 = (bf16[104,1024]{1,0:T(8,128)(2,1)S(1)}, bf16[104,1024]{1,0:T(8,128)(2,1)S(1)}) custom-call(s32[2]{0:T(128)S(1)} %copy-done.6, bf16[7,4,224,128]{3,2,1,0:T(8,128)(2,1)S(1)} %land.7.rows_ref, bf16[7,256,128]{2,1,0:T(8,128)(2,1)S(1)} %collective-permute-done.46.refs_0_, bf16[3,256,128]{2,1,0:T(8,128)(2,1)S(1)} %collective-permute-done.47.refs_1_, ...), custom_call_target="tpu_custom_call" | custom-call | flops 381681664 | bytes 2490368 | tf_op jit(solution)/shard_map/cond/branch_2_fun/expand/pallas_call | solution.py:338
  78.3 1.5 %collective-permute-start.50 = (bf16[104,1024]{1,0:T(8,128)(2,1)S(1)}, bf16[104,1024]{1,0:T(8,128)(2,1)S(1)}, u32[]{:S(2)}, u32[]{:S(2)}) collective-permute-start(bf16[104,1024]{1,0:T(8,128)(2,1)S(1)} %get-tuple-element.399), channel_id=1, source_target_pairs={{0,4},{4,0},{8,12},{12,8},{16,20},{20,16},{24,28},{28,24},{1,5},{5... | collective-permute-start | bytes 638984 | tf_op jit(solution)/shard_map/cond/branch_2_fun/ppermute | solution.py:211
  79.8 5.1 %collective-permute-done.50.refs_5_ = bf16[104,1024]{1,0:T(8,128)(2,1)S(1)} collective-permute-done((bf16[104,1024]{1,0:T(8,128)(2,1)S(1)}, bf16[104,1024]{1,0:T(8,128)(2,1)S(1)}, u32[]{:S(2)}, u32[]{:S(2)}) %collective-permute-start.50) | collective-permute-done | bytes 213024 | tf_op jit(solution)/shard_map/cond/branch_2_fun/ppermute | solution.py:211
  84.9 1.9 %join.7 = bf16[104,8192]{1,0:T(8,128)(2,1)} custom-call(s32[2]{0:T(128)S(1)} %copy-done.6, bf16[104,2048]{1,0:T(8,128)(2,1)S(1)} %expand_own.7.first_ref, bf16[104,1024]{1,0:T(8,128)(2,1)S(1)} %get-tuple-element.388.refs_0_, bf16[104,1024]{1,0:T(8,128)(2,1)S(1)} %get-tuple-element.390.refs_1_, bf16[104,1024]{1,0:T(8,128)(2,1)S(1)} %get-tuple-element.397.refs_2_, ...), custom_call_target="tpu_custom_call" | custom-call | bytes 3407872 | tf_op jit(solution)/shard_map/cond/branch_2_fun/join/pallas_call | solution.py:349
  (80 shorter events, 16.4 us)
Async XLA Ops:
  0.0 9.6 %copy-start.27 = (s32[5]{0:T(128)S(1)}, s32[5]{0:T(128)}, u32[]{:S(2)}) copy-start(s32[5]{0:T(128)} %param.37) | copy-start | bytes 64
  0.0 9.6 %copy-start.28 = (s32[5]{0:T(128)S(1)}, s32[5]{0:T(128)}, u32[]{:S(2)}) copy-start(s32[5]{0:T(128)} %param.36) | copy-start | bytes 64
  0.0 18.3 %copy-start = (bf16[10,256,128]{2,1,0:T(8,128)(2,1)S(1)}, bf16[10,256,128]{2,1,0:T(8,128)(2,1)}, u32[]{:S(2)}) copy-start(bf16[10,256,128]{2,1,0:T(8,128)(2,1)} %u_ref.1) | copy-start | bytes 1966084
  0.0 20.2 %collective-permute-start.86 = (bf16[5,256,128]{2,1,0:T(8,128)(2,1)}, bf16[5,256,128]{2,1,0:T(8,128)(2,1)}, u32[]{:S(2)}, u32[]{:S(2)}) collective-permute-start(bf16[5,256,128]{2,1,0:T(8,128)(2,1)} %param.33), channel_id=1, source_target_pairs={{0,8},{4,12},{8,0},{12,4},{16,24},{20,28},{24,16},{28,20},{1,9},{5... | collective-permute-start | bytes 983048 | tf_op jit(solution)/shard_map/ppermute | solution.py:208
  3.1 17.5 %collective-permute-start.87 = (bf16[5,256,128]{2,1,0:T(8,128)(2,1)}, bf16[5,256,128]{2,1,0:T(8,128)(2,1)}, u32[]{:S(2)}, u32[]{:S(2)}) collective-permute-start(bf16[5,256,128]{2,1,0:T(8,128)(2,1)} %param.33), channel_id=1, source_target_pairs={{0,16},{4,20},{8,24},{12,28},{16,0},{20,4},{24,8},{28,12},{1,17},{... | collective-permute-start | bytes 983048 | tf_op jit(solution)/shard_map/ppermute | solution.py:208
  5.8 14.8 %copy-start.21 = (s32[5]{0:T(128)S(1)}, s32[5]{0:T(128)}, u32[]{:S(2)}) copy-start(s32[5]{0:T(128)} %param.35) | copy-start | bytes 64
  5.8 14.8 %copy-start.22 = (s32[10]{0:T(128)S(1)}, s32[10]{0:T(128)}, u32[]{:S(2)}) copy-start(s32[10]{0:T(128)} %param.38) | copy-start | bytes 124
  8.1 12.5 %collective-permute-start.85 = (bf16[104,2048]{1,0:T(8,128)(2,1)S(1)}, bf16[104,2048]{1,0:T(8,128)(2,1)S(1)}, u32[]{:S(2)}, u32[]{:S(2)}) collective-permute-start(bf16[104,2048]{1,0:T(8,128)(2,1)S(1)} %get-tuple-element.494), channel_id=1, source_target_pairs={{0,4},{4,0},{8,12},{12,8},{16,20},{20,16},{24,28},{28,24},{1,5},{5... | collective-permute-start | bytes 1277960 | tf_op jit(solution)/shard_map/ppermute | solution.py:211
  9.6 3.6 %collective-permute-start.88 = (s32[5,2]{0,1:T(2,128)S(1)}, s32[5,2]{0,1:T(2,128)S(1)}, u32[]{:S(2)}, u32[]{:S(2)}) collective-permute-start(s32[5,2]{0,1:T(2,128)S(1)} %pad_add_fusion), channel_id=1, source_target_pairs={{0,2},{1,3},{2,0},{3,1},{4,6},{5,7},{6,4},{7,5},{8,10},{9,11},{10,... | collective-permute-start | bytes 128 | tf_op jit(solution)/shard_map/ppermute | solution.py:221
  13.3 1.1 %collective-permute-start.89 = (s32[10,2]{0,1:T(2,128)S(1)}, s32[10,2]{0,1:T(2,128)S(1)}, u32[]{:S(2)}, u32[]{:S(2)}) collective-permute-start(s32[10,2]{0,1:T(2,128)S(1)} %pad_add_fusion.1), channel_id=1, source_target_pairs={{0,1},{1,0},{2,3},{3,2},{4,5},{5,4},{6,7},{7,6},{8,9},{9,8},{10,11... | collective-permute-start | bytes 248 | tf_op jit(solution)/shard_map/ppermute | solution.py:221
  20.8 21.9 %copy-start.5 = (s32[2]{0:T(128)}, s32[2]{0:T(128)S(1)}, u32[]{:S(2)}) copy-start(s32[2]{0:T(128)S(1)} %get-tuple-element.367.pos_ref) | copy-start | bytes 28 | tf_op jit(solution)/shard_map/cond
  20.8 21.9 %copy-start.9 = (s32[10,20]{1,0:T(8,128)}, s32[10,20]{1,0:T(8,128)S(1)}, u32[]{:S(2)}) copy-start(s32[10,20]{1,0:T(8,128)S(1)} %get-tuple-element.535) | copy-start | bytes 2404 | tf_op jit(solution)/shard_map/cond
  20.9 21.9 %copy-start.13 = (pred[10,20]{1,0:T(8,128)(4,1)}, pred[10,20]{1,0:T(8,128)(4,1)S(1)}, u32[]{:S(2)}) copy-start(pred[10,20]{1,0:T(8,128)(4,1)S(1)} %get-tuple-element.534) | copy-start | bytes 604 | tf_op jit(solution)/shard_map/cond
  20.9 21.9 %copy-start.17 = (s32[10]{0:T(128)}, s32[10]{0:T(128)S(1)}, u32[]{:S(2)}) copy-start(s32[10]{0:T(128)S(1)} %get-tuple-element.370.offset_ref) | copy-start | bytes 124 | tf_op jit(solution)/shard_map/cond
  20.9 21.9 %copy-start.23 = (s32[10]{0:T(128)}, s32[10]{0:T(128)S(1)}, u32[]{:S(2)}) copy-start(s32[10]{0:T(128)S(1)} %get-tuple-element.545.target_ref) | copy-start | bytes 124 | tf_op jit(solution)/shard_map/cond
  20.9 19.3 %collective-permute-start.36 = (bf16[104,2048]{1,0:T(8,128)(2,1)}, bf16[104,2048]{1,0:T(8,128)(2,1)S(1)}, u32[]{:S(2)}, u32[]{:S(2)}) collective-permute-start(bf16[104,2048]{1,0:T(8,128)(2,1)} %get-tuple-element.375), channel_id=1, source_target_pairs={{0,4},{4,0},{8,12},{12,8},{16,20},{20,16},{24,28},{28,24},{1,5},{5... | collective-permute-start | bytes 1277960 | tf_op jit(solution)/shard_map/cond/branch_2_fun/ppermute | solution.py:211
  22.4 9.4 %collective-permute-start.37 = (bf16[5,256,128]{2,1,0:T(8,128)(2,1)}, bf16[5,256,128]{2,1,0:T(8,128)(2,1)S(1)}, u32[]{:S(2)}, u32[]{:S(2)}) collective-permute-start(bf16[5,256,128]{2,1,0:T(8,128)(2,1)} %get-tuple-element.376.refs_0_), channel_id=1, source_target_pairs={{8,16},{12,20},{16,8},{20,12},{9,17},{13,21},{17,9},{21,13},{10,18... | collective-permute-start | bytes 983048 | tf_op jit(solution)/shard_map/cond/branch_2_fun/ppermute | solution.py:208
  23.1 17.1 %collective-permute-start.38 = (bf16[5,256,128]{2,1,0:T(8,128)(2,1)}, bf16[5,256,128]{2,1,0:T(8,128)(2,1)S(1)}, u32[]{:S(2)}, u32[]{:S(2)}) collective-permute-start(bf16[5,256,128]{2,1,0:T(8,128)(2,1)} %get-tuple-element.378.refs_2_), channel_id=1, source_target_pairs={{8,0},{12,4},{16,24},{20,28},{9,1},{13,5},{17,25},{21,29},{10,2},{... | collective-permute-start | bytes 983048 | tf_op jit(solution)/shard_map/cond/branch_2_fun/ppermute | solution.py:208
  25.5 39.6 %collective-permute-start.43 = (bf16[7,256,128]{2,1,0:T(8,128)(2,1)S(1)}, bf16[7,256,128]{2,1,0:T(8,128)(2,1)S(1)}, u32[]{:S(2)}, u32[]{:S(2)}) collective-permute-start(bf16[7,256,128]{2,1,0:T(8,128)(2,1)S(1)} %slice.47.u_ref), channel_id=1, source_target_pairs={{0,8},{4,12},{8,0},{12,4},{16,24},{20,28},{24,16},{28,20},{1,9},{5... | collective-permute-start | bytes 1376264 | tf_op jit(solution)/shard_map/cond/branch_2_fun/ppermute | solution.py:208
  30.8 19.0 %collective-permute-start.41 = (bf16[3,256,128]{2,1,0:T(8,128)(2,1)S(1)}, bf16[3,256,128]{2,1,0:T(8,128)(2,1)S(1)}, u32[]{:S(2)}, u32[]{:S(2)}) collective-permute-start(bf16[3,256,128]{2,1,0:T(8,128)(2,1)S(1)} %slice.46), channel_id=1, source_target_pairs={{0,16},{4,20},{8,24},{12,28},{16,0},{20,4},{24,8},{28,12},{1,17},{... | collective-permute-start | bytes 589832 | tf_op jit(solution)/shard_map/cond/branch_2_fun/ppermute | solution.py:208
  42.8 5.2 %collective-permute-start.39 = (bf16[5,112,128]{2,1,0:T(8,128)(2,1)S(1)}, bf16[5,112,128]{2,1,0:T(8,128)(2,1)S(1)}, u32[]{:S(2)}, u32[]{:S(2)}) collective-permute-start(bf16[5,112,128]{2,1,0:T(8,128)(2,1)S(1)} %get-tuple-element.380), channel_id=1, source_target_pairs={{0,4},{4,0},{8,12},{12,8},{16,20},{20,16},{24,28},{28,24},{1,5},{5... | collective-permute-start | bytes 430088 | tf_op jit(solution)/shard_map/cond/branch_2_fun/ppermute | solution.py:211
  43.3 6.4 %collective-permute-start.40 = (bf16[5,112,128]{2,1,0:T(8,128)(2,1)S(1)}, bf16[5,112,128]{2,1,0:T(8,128)(2,1)S(1)}, u32[]{:S(2)}, u32[]{:S(2)}) collective-permute-start(bf16[5,112,128]{2,1,0:T(8,128)(2,1)S(1)} %get-tuple-element.381), channel_id=1, source_target_pairs={{0,4},{4,0},{8,12},{12,8},{16,20},{20,16},{24,28},{28,24},{1,5},{5... | collective-permute-start | bytes 430088 | tf_op jit(solution)/shard_map/cond/branch_2_fun/ppermute | solution.py:211
  45.0 16.8 %collective-permute-start.44 = (bf16[4,256,128]{2,1,0:T(8,128)(2,1)}, bf16[4,256,128]{2,1,0:T(8,128)(2,1)S(1)}, u32[]{:S(2)}, u32[]{:S(2)}) collective-permute-start(bf16[4,256,128]{2,1,0:T(8,128)(2,1)} %slice.48), channel_id=1, source_target_pairs={{0,16},{4,20},{8,24},{12,28},{16,0},{20,4},{24,8},{28,12},{1,17},{... | collective-permute-start | bytes 786440 | tf_op jit(solution)/shard_map/cond/branch_2_fun/ppermute | solution.py:208
  48.0 22.6 %collective-permute-start.42 = (bf16[7,256,128]{2,1,0:T(8,128)(2,1)S(1)}, bf16[7,256,128]{2,1,0:T(8,128)(2,1)S(1)}, u32[]{:S(2)}, u32[]{:S(2)}) collective-permute-start(bf16[7,256,128]{2,1,0:T(8,128)(2,1)S(1)} %slice.47.u_ref), channel_id=1, source_target_pairs={{0,4},{4,0},{8,12},{12,8},{16,20},{20,16},{24,28},{28,24},{1,5},{5... | collective-permute-start | bytes 1376264 | tf_op jit(solution)/shard_map/cond/branch_2_fun/ppermute | solution.py:211
  49.8 6.7 %collective-permute-start.34 = (bf16[5,2,112,128]{3,2,1,0:T(8,128)(2,1)S(1)}, bf16[5,2,112,128]{3,2,1,0:T(8,128)(2,1)S(1)}, u32[]{:S(2)}, u32[]{:S(2)}) collective-permute-start(bf16[5,2,112,128]{3,2,1,0:T(8,128)(2,1)S(1)} %get-tuple-element.876), channel_id=1, source_target_pairs={{0,2},{1,3},{2,0},{3,1},{4,6},{5,7},{6,4},{7,5},{8,10},{9,11},{10,... | collective-permute-start | bytes 860168 | tf_op jit(solution)/shard_map/cond/branch_2_fun/while/body/ppermute | solution.py:221
  57.5 2.3 %collective-permute-start.35 = (bf16[10,2,112,128]{3,2,1,0:T(8,128)(2,1)}, bf16[10,2,112,128]{3,2,1,0:T(8,128)(2,1)S(1)}, u32[]{:S(2)}, u32[]{:S(2)}) collective-permute-start(bf16[10,2,112,128]{3,2,1,0:T(8,128)(2,1)} %get-tuple-element.888), channel_id=1, source_target_pairs={{0,1},{1,0},{2,3},{3,2},{4,5},{5,4},{6,7},{7,6},{8,9},{9,8},{10,11... | collective-permute-start | bytes 1720328 | tf_op jit(solution)/shard_map/cond/branch_2_fun/while/body/ppermute | solution.py:221
  61.8 15.2 %collective-permute-start.46 = (bf16[7,256,128]{2,1,0:T(8,128)(2,1)S(1)}, bf16[7,256,128]{2,1,0:T(8,128)(2,1)S(1)}, u32[]{:S(2)}, u32[]{:S(2)}) collective-permute-start(bf16[7,256,128]{2,1,0:T(8,128)(2,1)S(1)} %slice.47.u_ref), channel_id=1, source_target_pairs={{8,16},{12,20},{16,8},{20,12},{9,17},{13,21},{17,9},{21,13},{10,18... | collective-permute-start | bytes 1376264 | tf_op jit(solution)/shard_map/cond/branch_2_fun/ppermute | solution.py:208
  62.5 14.5 %collective-permute-start.48 = (bf16[4,256,128]{2,1,0:T(8,128)(2,1)S(1)}, bf16[4,256,128]{2,1,0:T(8,128)(2,1)S(1)}, u32[]{:S(2)}, u32[]{:S(2)}) collective-permute-start(bf16[4,256,128]{2,1,0:T(8,128)(2,1)S(1)} %collective-permute-done.44.refs_1_), channel_id=1, source_target_pairs={{8,0},{12,4},{16,24},{20,28},{9,1},{13,5},{17,25},{21,29},{10,2},{... | collective-permute-start | bytes 786440 | tf_op jit(solution)/shard_map/cond/branch_2_fun/ppermute | solution.py:208
  66.4 8.0 %collective-permute-start.45 = (bf16[104,1024]{1,0:T(8,128)(2,1)S(1)}, bf16[104,1024]{1,0:T(8,128)(2,1)S(1)}, u32[]{:S(2)}, u32[]{:S(2)}) collective-permute-start(bf16[104,1024]{1,0:T(8,128)(2,1)S(1)} %get-tuple-element.392), channel_id=1, source_target_pairs={{0,4},{4,0},{8,12},{12,8},{16,20},{20,16},{24,28},{28,24},{1,5},{5... | collective-permute-start | bytes 638984 | tf_op jit(solution)/shard_map/cond/branch_2_fun/ppermute | solution.py:211
  68.0 9.0 %collective-permute-start.47 = (bf16[3,256,128]{2,1,0:T(8,128)(2,1)S(1)}, bf16[3,256,128]{2,1,0:T(8,128)(2,1)S(1)}, u32[]{:S(2)}, u32[]{:S(2)}) collective-permute-start(bf16[3,256,128]{2,1,0:T(8,128)(2,1)S(1)} %collective-permute-done.41.refs_0_), channel_id=1, source_target_pairs={{8,0},{12,4},{16,24},{20,28},{9,1},{13,5},{17,25},{21,29},{10,2},{... | collective-permute-start | bytes 589832 | tf_op jit(solution)/shard_map/cond/branch_2_fun/ppermute | solution.py:208
  70.6 9.2 %collective-permute-start.49 = (bf16[104,1024]{1,0:T(8,128)(2,1)S(1)}, bf16[104,1024]{1,0:T(8,128)(2,1)S(1)}, u32[]{:S(2)}, u32[]{:S(2)}) collective-permute-start(bf16[104,1024]{1,0:T(8,128)(2,1)S(1)} %get-tuple-element.398), channel_id=1, source_target_pairs={{0,4},{4,0},{8,12},{12,8},{16,20},{20,16},{24,28},{28,24},{1,5},{5... | collective-permute-start | bytes 638984 | tf_op jit(solution)/shard_map/cond/branch_2_fun/ppermute | solution.py:211
  78.3 6.6 %collective-permute-start.50 = (bf16[104,1024]{1,0:T(8,128)(2,1)S(1)}, bf16[104,1024]{1,0:T(8,128)(2,1)S(1)}, u32[]{:S(2)}, u32[]{:S(2)}) collective-permute-start(bf16[104,1024]{1,0:T(8,128)(2,1)S(1)} %get-tuple-element.399), channel_id=1, source_target_pairs={{0,4},{4,0},{8,12},{12,8},{16,20},{20,16},{24,28},{28,24},{1,5},{5... | collective-permute-start | bytes 638984 | tf_op jit(solution)/shard_map/cond/branch_2_fun/ppermute | solution.py:211
  (5 other events, 14.2 us)

commit v2 on v0

--- a/solution.py
+++ b/solution.py
@@ -260,7 +260,7 @@
 
     x_low, x_high = [across(part) for part in packed]
     v_ends = move(after(v_far, *packed), ends)
-    v_middle = move(after(v_factors, v_far), middle)
+    v_middle = move(v_factors, middle)
     arrived = lax.optimization_barrier(
         (x_low, x_high, v_near, v_far, v_middle, v_ends, squeezed, level)
     )

time: 81.8 us -> 77.6 us (0.949)
  starting transfers between devices: 27.9 us -> 25.3 us
  waiting for transfers between devices: 34.5 us -> 32.5 us
    ppermute x8, waiting for transfers between devices: 13 us -> 7.58 us  [move(): lax.ppermute(array, 'rhs', [(2 * a + i, 2 * b + i) for a, b in pairs for...]
    ppermute x7, waiting for transfers between devices: 11.1 us -> 14.7 us  [across(): return lax.ppermute(array, 'rhs', [(p, p ^ 1) for p in range(2 * PLACES)])]
    ppermute x8, starting transfers between devices: 18 us -> 14.5 us  [move(): lax.ppermute(array, 'rhs', [(2 * a + i, 2 * b + i) for a, b in pairs for...]
    ppermute x7, starting transfers between devices: 6.76 us -> 7.65 us  [across(): return lax.ppermute(array, 'rhs', [(p, p ^ 1) for p in range(2 * PLACES)])]
  transfers between devices with their start and end apart: 19 -> 19, of which waited for: 11 -> 13; matrix products, arithmetic and copies ran while one was open for 2% -> 3% of each run, Pallas kernels for 10% -> 11%
where the time goes in v2:
time: 77.6 us; the launch traced here: 76.4 us
  waiting for transfers between devices  32.5 us (42%)
  starting transfers between devices  25.3 us (33%)
  Pallas kernels  11.8 us (15%)
  between operations  2.69 us (3%)
  other arithmetic  1.88 us (2%)
  local copies, waits for them, and re-layouts  1.36 us (2%)
  loops' own time  0.88 us (1%)
    ppermute x7, waiting for transfers between devices, across(): return lax.ppermute(array, 'rhs', [(p, p ^ 1) for p in range(2 * PLACES)])  14.7 us
    ppermute x8, starting transfers between devices, move(): lax.ppermute(array, 'rhs', [(2 * a + i, 2 * b + i) for a, b in pairs for...  14.5 us
    ppermute x4, waiting for transfers between devices, swapped(): return lax.ppermute(array, 'clus', [(p, p ^ stage) for p in range(owners)])  10.2 us
    ppermute x7, starting transfers between devices, across(): return lax.ppermute(array, 'rhs', [(p, p ^ 1) for p in range(2 * PLACES)])  7.65 us
    ppermute x8, waiting for transfers between devices, move(): lax.ppermute(array, 'rhs', [(2 * a + i, 2 * b + i) for a, b in pairs for...  7.58 us
    pallas_call x3, Pallas kernels, rest(): call(functools.partial(expand_body, seg, columns), [chunk, chunk], [SMEM,...  3.46 us
    ppermute x4, starting transfers between devices, swapped(): return lax.ppermute(array, 'clus', [(p, p ^ stage) for p in range(owners)])  3.18 us
    pallas_call x1, Pallas kernels, rest(): call(functools.partial(compress_body, seg), [jax.ShapeDtypeStruct((blocks...  2.68 us
  transfers between devices with their start and end apart: 19, of which 13 were waited for; matrix products, arithmetic and copies ran while one was open for 3% of the time, Pallas kernels for 11%

profile of v2, /device:TPU:0, one launch (start us, length us, event | category | flops | bytes accessed | tf_op | source)
XLA Modules:
  0.0 76.4 jit_solution(16432804752065285941)
XLA Ops:
  0.0 4.1 %collective-permute-start.58 = (bf16[5,256,128]{2,1,0:T(8,128)(2,1)}, bf16[5,256,128]{2,1,0:T(8,128)(2,1)}, u32[]{:S(2)}, u32[]{:S(2)}) collective-permute-start(bf16[5,256,128]{2,1,0:T(8,128)(2,1)} %param.33), channel_id=1, source_target_pairs={{0,16},{4,20},{8,24},{12,28},{16,0},{20,4},{24,8},{28,12},{1,17},{... | collective-permute-start | bytes 983048 | tf_op jit(solution)/shard_map/ppermute | solution.py:206
  4.1 1.6 %collective-permute-start.57 = (bf16[5,256,128]{2,1,0:T(8,128)(2,1)}, bf16[5,256,128]{2,1,0:T(8,128)(2,1)}, u32[]{:S(2)}, u32[]{:S(2)}) collective-permute-start(bf16[5,256,128]{2,1,0:T(8,128)(2,1)} %param.33), channel_id=1, source_target_pairs={{0,8},{4,12},{8,0},{12,4},{16,24},{20,28},{24,16},{28,20},{1,9},{5... | collective-permute-start | bytes 983048 | tf_op jit(solution)/shard_map/ppermute | solution.py:206
  5.7 1.4 %collective-permute-start.59 = (bf16[5,256,128]{2,1,0:T(8,128)(2,1)}, bf16[5,256,128]{2,1,0:T(8,128)(2,1)}, u32[]{:S(2)}, u32[]{:S(2)}) collective-permute-start(bf16[5,256,128]{2,1,0:T(8,128)(2,1)} %param.33), channel_id=1, source_target_pairs={{8,16},{12,20},{16,8},{20,12},{9,17},{13,21},{17,9},{21,13},{10,18... | collective-permute-start | bytes 983048 | tf_op jit(solution)/shard_map/ppermute | solution.py:206
  7.1 1.6 %pack.1 = (bf16[104,2048]{1,0:T(8,128)(2,1)S(1)}, bf16[104,2048]{1,0:T(8,128)(2,1)S(1)}) custom-call(s32[2]{0:T(128)S(1)} %pad_add_fusion.3.pos_ref, bf16[104,8192]{1,0:T(8,128)(2,1)} %x_ref.1), custom_call_target="tpu_custom_call" | custom-call | bytes 2555904 | tf_op jit(solution)/shard_map/pack/pallas_call | solution.py:225
  8.8 1.6 %collective-permute-start.55 = (bf16[104,2048]{1,0:T(8,128)(2,1)S(1)}, bf16[104,2048]{1,0:T(8,128)(2,1)S(1)}, u32[]{:S(2)}, u32[]{:S(2)}) collective-permute-start(bf16[104,2048]{1,0:T(8,128)(2,1)S(1)} %get-tuple-element.512), channel_id=1, source_target_pairs={{0,4},{4,0},{8,12},{12,8},{16,20},{20,16},{24,28},{28,24},{1,5},{5... | collective-permute-start | bytes 1277960 | tf_op jit(solution)/shard_map/ppermute | solution.py:209
  10.3 1.6 %collective-permute-start.61 = (s32[5,2]{0,1:T(2,128)S(1)}, s32[5,2]{0,1:T(2,128)S(1)}, u32[]{:S(2)}, u32[]{:S(2)}) collective-permute-start(s32[5,2]{0,1:T(2,128)S(1)} %pad_add_fusion), channel_id=1, source_target_pairs={{0,2},{1,3},{2,0},{3,1},{4,6},{5,7},{6,4},{7,5},{8,10},{9,11},{10,... | collective-permute-start | bytes 128 | tf_op jit(solution)/shard_map/ppermute | solution.py:219
  11.9 2.0 %collective-permute-done.61 = s32[5,2]{0,1:T(2,128)S(1)} collective-permute-done((s32[5,2]{0,1:T(2,128)S(1)}, s32[5,2]{0,1:T(2,128)S(1)}, u32[]{:S(2)}, u32[]{:S(2)}) %collective-permute-start.61) | collective-permute-done | bytes 72 | tf_op jit(solution)/shard_map/ppermute | solution.py:219
  20.0 1.3 %collective-permute-start.60 = (bf16[5,256,128]{2,1,0:T(8,128)(2,1)}, bf16[5,256,128]{2,1,0:T(8,128)(2,1)}, u32[]{:S(2)}, u32[]{:S(2)}) collective-permute-start(bf16[5,256,128]{2,1,0:T(8,128)(2,1)} %collective-permute-done.58), channel_id=1, source_target_pairs={{8,0},{12,4},{16,24},{20,28},{9,1},{13,5},{17,25},{21,29},{10,2},{... | collective-permute-start | bytes 983048 | tf_op jit(solution)/shard_map/ppermute | solution.py:206
  22.6 6.4 %collective-permute-done.56 = bf16[104,2048]{1,0:T(8,128)(2,1)S(1)} collective-permute-done((bf16[104,2048]{1,0:T(8,128)(2,1)S(1)}, bf16[104,2048]{1,0:T(8,128)(2,1)S(1)}, u32[]{:S(2)}, u32[]{:S(2)}) %collective-permute-start.56) | collective-permute-done | bytes 426016 | tf_op jit(solution)/shard_map/ppermute | solution.py:209
  29.0 2.2 %collective-permute-done.60 = bf16[5,256,128]{2,1,0:T(8,128)(2,1)} collective-permute-done((bf16[5,256,128]{2,1,0:T(8,128)(2,1)}, bf16[5,256,128]{2,1,0:T(8,128)(2,1)}, u32[]{:S(2)}, u32[]{:S(2)}) %collective-permute-start.60) | collective-permute-done | bytes 327712 | tf_op jit(solution)/shard_map/ppermute | solution.py:206
  31.2 44.0 %conditional.1 = (bf16[104,8192]{1,0:T(8,128)(2,1)S(1)}) conditional(s32[]{:T(128)} %clamp.3, (s32[5]{0:T(128)S(1)}, s32[2]{0:T(128)S(1)}, s32[5]{0:T(128)S(1)}, bf16[104,8192]{1,0:T(8,128)(2,1)}, bf16[104,2048]{1,0:T(8,128)(2,1)S(1)}, /*index=5*/bf16[104,2048]{1,0:T(8,128)(2,1)S(1)}, ...), branch_computations={%region_5.10_spmd, %region_10.15_spmd, %region_15.20_spmd, %region... | conditional | flops 2455675904 | bytes 55446488 | solution.py:348
  31.3 2.7 %compress.6 = (f32[5,2,112,128]{3,2,1,0:T(8,128)S(1)}, bf16[5,2,112,128]{3,2,1,0:T(8,128)(2,1)S(1)}) custom-call(s32[2]{0:T(128)S(1)} %get-tuple-element.343.pos_ref, s32[5]{0:T(128)S(1)} %get-tuple-element.545.source_ref, bf16[104,8192]{1,0:T(8,128)(2,1)} %get-tuple-element.349.x_ref, bf16[104,2048]{1,0:T(8,128)(2,1)S(1)} %get-tuple-element.350.xl_ref, ...), custom_call_target="tpu_custom_call" | custom-call | flops 272629760 | bytes 3866624 | tf_op jit(solution)/shard_map/cond/branch_1_fun/compress/pallas_call | solution.py:271
  34.0 1.6 %collective-permute-start.35 = (bf16[5,2,112,128]{3,2,1,0:T(8,128)(2,1)S(1)}, bf16[5,2,112,128]{3,2,1,0:T(8,128)(2,1)S(1)}, u32[]{:S(2)}, u32[]{:S(2)}) collective-permute-start(bf16[5,2,112,128]{3,2,1,0:T(8,128)(2,1)S(1)} %get-tuple-element.358), channel_id=1, source_target_pairs={{0,4},{4,0},{8,12},{12,8},{16,20},{20,16},{24,28},{28,24},{1,5},{5... | collective-permute-start | bytes 860168 | tf_op jit(solution)/shard_map/cond/branch_1_fun/ppermute | solution.py:209
  35.7 3.9 %collective-permute-start.38 = (bf16[6,256,128]{2,1,0:T(8,128)(2,1)S(1)}, bf16[6,256,128]{2,1,0:T(8,128)(2,1)S(1)}, u32[]{:S(2)}, u32[]{:S(2)}) collective-permute-start(bf16[6,256,128]{2,1,0:T(8,128)(2,1)S(1)} %slice.13.u_ref), channel_id=1, source_target_pairs={{0,16},{4,20},{8,24},{12,28},{16,0},{20,4},{24,8},{28,12},{1,17},{... | collective-permute-start | bytes 1179656 | tf_op jit(solution)/shard_map/cond/branch_1_fun/ppermute | solution.py:206
  39.6 1.5 %collective-permute-done.35 = bf16[5,2,112,128]{3,2,1,0:T(8,128)(2,1)S(1)} collective-permute-done((bf16[5,2,112,128]{3,2,1,0:T(8,128)(2,1)S(1)}, bf16[5,2,112,128]{3,2,1,0:T(8,128)(2,1)S(1)}, u32[]{:S(2)}, u32[]{:S(2)}) %collective-permute-start.35) | collective-permute-done | bytes 286752 | tf_op jit(solution)/shard_map/cond/branch_1_fun/ppermute | solution.py:209
  41.3 1.2 %collective-permute-start.36 = (bf16[6,256,128]{2,1,0:T(8,128)(2,1)S(1)}, bf16[6,256,128]{2,1,0:T(8,128)(2,1)S(1)}, u32[]{:S(2)}, u32[]{:S(2)}) collective-permute-start(bf16[6,256,128]{2,1,0:T(8,128)(2,1)S(1)} %slice.13.u_ref), channel_id=1, source_target_pairs={{0,4},{4,0},{8,12},{12,8},{16,20},{20,16},{24,28},{28,24},{1,5},{5... | collective-permute-start | bytes 1179656 | tf_op jit(solution)/shard_map/cond/branch_1_fun/ppermute | solution.py:209
  42.6 6.7 %while.92 = (s32[]{:T(128)}, bf16[5,2,112,128]{3,2,1,0:T(8,128)(2,1)S(1)}, s32[]{:T(128)}, s32[]{:T(128)}) while((s32[]{:T(128)}, bf16[5,2,112,128]{3,2,1,0:T(8,128)(2,1)S(1)}, s32[]{:T(128)}, s32[]{:T(128)}) %tuple.200), condition=%wide.region_12.12_spmd, body=%wide.region_11.11_spmd.sunk | while | flops 2 | bytes 1720413 | solution.py:297
  42.6 1.5 %collective-permute-start.33 = (bf16[5,2,112,128]{3,2,1,0:T(8,128)(2,1)S(1)}, bf16[5,2,112,128]{3,2,1,0:T(8,128)(2,1)S(1)}, u32[]{:S(2)}, u32[]{:S(2)}) collective-permute-start(bf16[5,2,112,128]{3,2,1,0:T(8,128)(2,1)S(1)} %get-tuple-element.915), channel_id=1, source_target_pairs={{0,2},{1,3},{2,0},{3,1},{4,6},{5,7},{6,4},{7,5},{8,10},{9,11},{10,... | collective-permute-start | bytes 860168 | tf_op jit(solution)/shard_map/cond/branch_1_fun/while/body/ppermute | solution.py:219
  44.1 5.1 %collective-permute-done.33 = bf16[5,2,112,128]{3,2,1,0:T(8,128)(2,1)S(1)} collective-permute-done((bf16[5,2,112,128]{3,2,1,0:T(8,128)(2,1)S(1)}, bf16[5,2,112,128]{3,2,1,0:T(8,128)(2,1)S(1)}, u32[]{:S(2)}, u32[]{:S(2)}) %collective-permute-start.33) | collective-permute-done | bytes 286752 | tf_op jit(solution)/shard_map/cond/branch_1_fun/while/body/ppermute | solution.py:219
  49.3 2.1 %while.93 = (s32[]{:T(128)}, bf16[10,2,112,128]{3,2,1,0:T(8,128)(2,1)S(1)}, s32[]{:T(128)}, s32[]{:T(128)}) while((s32[]{:T(128)}, bf16[10,2,112,128]{3,2,1,0:T(8,128)(2,1)S(1)}, s32[]{:T(128)}, s32[]{:T(128)}) %tuple.203), condition=%wide.region_14.14_spmd, body=%wide.region_13.13_spmd.sunk | while | flops 2 | bytes 3440733 | solution.py:297
  49.4 2.0 %collective-permute-done.34 = bf16[10,2,112,128]{3,2,1,0:T(8,128)(2,1)S(1)} collective-permute-done((bf16[10,2,112,128]{3,2,1,0:T(8,128)(2,1)S(1)}, bf16[10,2,112,128]{3,2,1,0:T(8,128)(2,1)S(1)}, u32[]{:S(2)}, u32[]{:S(2)}) %collective-permute-start.34) | collective-permute-done | bytes 573472 | tf_op jit(solution)/shard_map/cond/branch_1_fun/while/body/ppermute | solution.py:219
  51.6 4.3 %collective-permute-done.38.refs_0_ = bf16[6,256,128]{2,1,0:T(8,128)(2,1)S(1)} collective-permute-done((bf16[6,256,128]{2,1,0:T(8,128)(2,1)S(1)}, bf16[6,256,128]{2,1,0:T(8,128)(2,1)S(1)}, u32[]{:S(2)}, u32[]{:S(2)}) %collective-permute-start.38) | collective-permute-done | bytes 393248 | tf_op jit(solution)/shard_map/cond/branch_1_fun/ppermute | solution.py:206
  56.5 1.5 %collective-permute-start.41 = (bf16[6,256,128]{2,1,0:T(8,128)(2,1)S(1)}, bf16[6,256,128]{2,1,0:T(8,128)(2,1)S(1)}, u32[]{:S(2)}, u32[]{:S(2)}) collective-permute-start(bf16[6,256,128]{2,1,0:T(8,128)(2,1)S(1)} %collective-permute-done.38.refs_0_), channel_id=1, source_target_pairs={{8,0},{12,4},{16,24},{20,28},{9,1},{13,5},{17,25},{21,29},{10,2},{... | collective-permute-start | bytes 1179656 | tf_op jit(solution)/shard_map/cond/branch_1_fun/ppermute | solution.py:206
  58.2 1.1 %land.6.rows_ref = bf16[6,4,224,128]{3,2,1,0:T(8,128)(2,1)S(1)} custom-call(s32[10]{0:T(128)S(1)} %select_reduce_fusion.1.index_ref, s32[10]{0:T(128)S(1)} %copy-done.15, s32[10]{0:T(128)S(1)} %copy-done.11, bf16[20,2,112,128]{3,2,1,0:T(8,128)(2,1)S(1)} %pad_maximum_fusion.2.comp_ref), custom_call_target="tpu_custom_call" | custom-call | bytes 5734400 | tf_op jit(solution)/shard_map/cond/branch_1_fun/land/pallas_call | solution.py:303
  59.3 1.2 %expand.18 = (bf16[104,1024]{1,0:T(8,128)(2,1)S(1)}, bf16[104,1024]{1,0:T(8,128)(2,1)S(1)}) custom-call(s32[2]{0:T(128)S(1)} %copy-done.5, bf16[6,4,224,128]{3,2,1,0:T(8,128)(2,1)S(1)} %land.6.rows_ref, bf16[6,256,128]{2,1,0:T(8,128)(2,1)S(1)} %collective-permute-done.37.refs_0_), custom_call_target="tpu_custom_call" | custom-call | flops 327155712 | bytes 2195456 | tf_op jit(solution)/shard_map/cond/branch_1_fun/expand/pallas_call | solution.py:329
  61.1 1.1 %expand.19 = (bf16[104,1024]{1,0:T(8,128)(2,1)S(1)}, bf16[104,1024]{1,0:T(8,128)(2,1)S(1)}) custom-call(s32[2]{0:T(128)S(1)} %copy-done.5, bf16[6,4,224,128]{3,2,1,0:T(8,128)(2,1)S(1)} %land.6.rows_ref, bf16[6,256,128]{2,1,0:T(8,128)(2,1)S(1)} %collective-permute-done.38.refs_0_), custom_call_target="tpu_custom_call" | custom-call | flops 327155712 | bytes 2195456 | tf_op jit(solution)/shard_map/cond/branch_1_fun/expand/pallas_call | solution.py:329
  62.2 1.6 %collective-permute-start.42 = (bf16[104,1024]{1,0:T(8,128)(2,1)S(1)}, bf16[104,1024]{1,0:T(8,128)(2,1)S(1)}, u32[]{:S(2)}, u32[]{:S(2)}) collective-permute-start(bf16[104,1024]{1,0:T(8,128)(2,1)S(1)} %get-tuple-element.373), channel_id=1, source_target_pairs={{0,4},{4,0},{8,12},{12,8},{16,20},{20,16},{24,28},{28,24},{1,5},{5... | collective-permute-start | bytes 638984 | tf_op jit(solution)/shard_map/cond/branch_1_fun/ppermute | solution.py:209
  64.9 1.5 %collective-permute-done.39.refs_3_ = bf16[104,1024]{1,0:T(8,128)(2,1)S(1)} collective-permute-done((bf16[104,1024]{1,0:T(8,128)(2,1)S(1)}, bf16[104,1024]{1,0:T(8,128)(2,1)S(1)}, u32[]{:S(2)}, u32[]{:S(2)}) %collective-permute-start.39) | collective-permute-done | bytes 213024 | tf_op jit(solution)/shard_map/cond/branch_1_fun/ppermute | solution.py:209
  66.9 1.2 %expand.20 = (bf16[104,1024]{1,0:T(8,128)(2,1)S(1)}, bf16[104,1024]{1,0:T(8,128)(2,1)S(1)}) custom-call(s32[2]{0:T(128)S(1)} %copy-done.5, bf16[6,4,224,128]{3,2,1,0:T(8,128)(2,1)S(1)} %land.6.rows_ref, bf16[6,256,128]{2,1,0:T(8,128)(2,1)S(1)} %collective-permute-done.40.refs_0_, bf16[6,256,128]{2,1,0:T(8,128)(2,1)S(1)} %collective-permute-done.41.refs_1_), custom_call_target="tpu_custom_call" | custom-call | flops 327155712 | bytes 2195456 | tf_op jit(solution)/shard_map/cond/branch_1_fun/expand/pallas_call | solution.py:329
  68.7 1.4 %collective-permute-done.42.refs_4_ = bf16[104,1024]{1,0:T(8,128)(2,1)S(1)} collective-permute-done((bf16[104,1024]{1,0:T(8,128)(2,1)S(1)}, bf16[104,1024]{1,0:T(8,128)(2,1)S(1)}, u32[]{:S(2)}, u32[]{:S(2)}) %collective-permute-start.42) | collective-permute-done | bytes 213024 | tf_op jit(solution)/shard_map/cond/branch_1_fun/ppermute | solution.py:209
  70.0 3.9 %collective-permute-done.43.refs_5_ = bf16[104,1024]{1,0:T(8,128)(2,1)S(1)} collective-permute-done((bf16[104,1024]{1,0:T(8,128)(2,1)S(1)}, bf16[104,1024]{1,0:T(8,128)(2,1)S(1)}, u32[]{:S(2)}, u32[]{:S(2)}) %collective-permute-start.43) | collective-permute-done | bytes 213024 | tf_op jit(solution)/shard_map/cond/branch_1_fun/ppermute | solution.py:209
  75.2 1.2 %copy-done.3 = bf16[104,8192]{1,0:T(8,128)(2,1)} copy-done((bf16[104,8192]{1,0:T(8,128)(2,1)}, bf16[104,8192]{1,0:T(8,128)(2,1)S(1)}, u32[]{:S(2)}) %copy-start.3) | copy-done | bytes 1703960
  (74 shorter events, 9.7 us)
Async XLA Ops:
  0.0 10.3 %copy-start.16 = (s32[5]{0:T(128)S(1)}, s32[5]{0:T(128)}, u32[]{:S(2)}) copy-start(s32[5]{0:T(128)} %param.37) | copy-start | bytes 64
  0.0 10.3 %copy-start.17 = (s32[5]{0:T(128)S(1)}, s32[5]{0:T(128)}, u32[]{:S(2)}) copy-start(s32[5]{0:T(128)} %param.36) | copy-start | bytes 64
  0.0 21.4 %copy-start = (bf16[10,256,128]{2,1,0:T(8,128)(2,1)S(1)}, bf16[10,256,128]{2,1,0:T(8,128)(2,1)}, u32[]{:S(2)}) copy-start(bf16[10,256,128]{2,1,0:T(8,128)(2,1)} %u_ref.1) | copy-start | bytes 1966084
  0.0 20.0 %collective-permute-start.58 = (bf16[5,256,128]{2,1,0:T(8,128)(2,1)}, bf16[5,256,128]{2,1,0:T(8,128)(2,1)}, u32[]{:S(2)}, u32[]{:S(2)}) collective-permute-start(bf16[5,256,128]{2,1,0:T(8,128)(2,1)} %param.33), channel_id=1, source_target_pairs={{0,16},{4,20},{8,24},{12,28},{16,0},{20,4},{24,8},{28,12},{1,17},{... | collective-permute-start | bytes 983048 | tf_op jit(solution)/shard_map/ppermute | solution.py:206
  4.1 18.5 %collective-permute-start.57 = (bf16[5,256,128]{2,1,0:T(8,128)(2,1)}, bf16[5,256,128]{2,1,0:T(8,128)(2,1)}, u32[]{:S(2)}, u32[]{:S(2)}) collective-permute-start(bf16[5,256,128]{2,1,0:T(8,128)(2,1)} %param.33), channel_id=1, source_target_pairs={{0,8},{4,12},{8,0},{12,4},{16,24},{20,28},{24,16},{28,20},{1,9},{5... | collective-permute-start | bytes 983048 | tf_op jit(solution)/shard_map/ppermute | solution.py:206
  5.7 16.9 %collective-permute-start.59 = (bf16[5,256,128]{2,1,0:T(8,128)(2,1)}, bf16[5,256,128]{2,1,0:T(8,128)(2,1)}, u32[]{:S(2)}, u32[]{:S(2)}) collective-permute-start(bf16[5,256,128]{2,1,0:T(8,128)(2,1)} %param.33), channel_id=1, source_target_pairs={{8,16},{12,20},{16,8},{20,12},{9,17},{13,21},{17,9},{21,13},{10,18... | collective-permute-start | bytes 983048 | tf_op jit(solution)/shard_map/ppermute | solution.py:206
  7.1 24.0 %copy-start.1 = (bf16[5,256,128]{2,1,0:T(8,128)(2,1)S(1)}, bf16[5,256,128]{2,1,0:T(8,128)(2,1)}, u32[]{:S(2)}) copy-start(bf16[5,256,128]{2,1,0:T(8,128)(2,1)} %param.33) | copy-start | bytes 983044
  7.1 24.0 %copy-start.12 = (s32[5]{0:T(128)S(1)}, s32[5]{0:T(128)}, u32[]{:S(2)}) copy-start(s32[5]{0:T(128)} %param.35) | copy-start | bytes 64
  7.1 24.0 %copy-start.13 = (s32[10]{0:T(128)S(1)}, s32[10]{0:T(128)}, u32[]{:S(2)}) copy-start(s32[10]{0:T(128)} %param.38) | copy-start | bytes 124
  8.8 13.8 %collective-permute-start.55 = (bf16[104,2048]{1,0:T(8,128)(2,1)S(1)}, bf16[104,2048]{1,0:T(8,128)(2,1)S(1)}, u32[]{:S(2)}, u32[]{:S(2)}) collective-permute-start(bf16[104,2048]{1,0:T(8,128)(2,1)S(1)} %get-tuple-element.512), channel_id=1, source_target_pairs={{0,4},{4,0},{8,12},{12,8},{16,20},{20,16},{24,28},{28,24},{1,5},{5... | collective-permute-start | bytes 1277960 | tf_op jit(solution)/shard_map/ppermute | solution.py:209
  10.3 3.6 %collective-permute-start.61 = (s32[5,2]{0,1:T(2,128)S(1)}, s32[5,2]{0,1:T(2,128)S(1)}, u32[]{:S(2)}, u32[]{:S(2)}) collective-permute-start(s32[5,2]{0,1:T(2,128)S(1)} %pad_add_fusion), channel_id=1, source_target_pairs={{0,2},{1,3},{2,0},{3,1},{4,6},{5,7},{6,4},{7,5},{8,10},{9,11},{10,... | collective-permute-start | bytes 128 | tf_op jit(solution)/shard_map/ppermute | solution.py:219
  14.1 1.1 %collective-permute-start.62 = (s32[10,2]{0,1:T(2,128)S(1)}, s32[10,2]{0,1:T(2,128)S(1)}, u32[]{:S(2)}, u32[]{:S(2)}) collective-permute-start(s32[10,2]{0,1:T(2,128)S(1)} %pad_add_fusion.1), channel_id=1, source_target_pairs={{0,1},{1,0},{2,3},{3,2},{4,5},{5,4},{6,7},{7,6},{8,9},{9,8},{10,11... | collective-permute-start | bytes 248 | tf_op jit(solution)/shard_map/ppermute | solution.py:219
  15.2 13.8 %collective-permute-start.56 = (bf16[104,2048]{1,0:T(8,128)(2,1)S(1)}, bf16[104,2048]{1,0:T(8,128)(2,1)S(1)}, u32[]{:S(2)}, u32[]{:S(2)}) collective-permute-start(bf16[104,2048]{1,0:T(8,128)(2,1)S(1)} %get-tuple-element.513), channel_id=1, source_target_pairs={{0,4},{4,0},{8,12},{12,8},{16,20},{20,16},{24,28},{28,24},{1,5},{5... | collective-permute-start | bytes 1277960 | tf_op jit(solution)/shard_map/ppermute | solution.py:209
  20.0 11.1 %collective-permute-start.60 = (bf16[5,256,128]{2,1,0:T(8,128)(2,1)}, bf16[5,256,128]{2,1,0:T(8,128)(2,1)}, u32[]{:S(2)}, u32[]{:S(2)}) collective-permute-start(bf16[5,256,128]{2,1,0:T(8,128)(2,1)} %collective-permute-done.58), channel_id=1, source_target_pairs={{8,0},{12,4},{16,24},{20,28},{9,1},{13,5},{17,25},{21,29},{10,2},{... | collective-permute-start | bytes 983048 | tf_op jit(solution)/shard_map/ppermute | solution.py:206
  31.2 2.7 %copy-start.4 = (s32[2]{0:T(128)}, s32[2]{0:T(128)S(1)}, u32[]{:S(2)}) copy-start(s32[2]{0:T(128)S(1)} %get-tuple-element.343.pos_ref) | copy-start | bytes 28 | tf_op jit(solution)/shard_map/cond
  31.2 2.7 %copy-start.6 = (s32[10,20]{1,0:T(8,128)}, s32[10,20]{1,0:T(8,128)S(1)}, u32[]{:S(2)}) copy-start(s32[10,20]{1,0:T(8,128)S(1)} %get-tuple-element.553) | copy-start | bytes 2404 | tf_op jit(solution)/shard_map/cond
  31.2 2.7 %copy-start.8 = (pred[10,20]{1,0:T(8,128)(4,1)}, pred[10,20]{1,0:T(8,128)(4,1)S(1)}, u32[]{:S(2)}) copy-start(pred[10,20]{1,0:T(8,128)(4,1)S(1)} %get-tuple-element.552) | copy-start | bytes 604 | tf_op jit(solution)/shard_map/cond
  34.0 7.2 %collective-permute-start.35 = (bf16[5,2,112,128]{3,2,1,0:T(8,128)(2,1)S(1)}, bf16[5,2,112,128]{3,2,1,0:T(8,128)(2,1)S(1)}, u32[]{:S(2)}, u32[]{:S(2)}) collective-permute-start(bf16[5,2,112,128]{3,2,1,0:T(8,128)(2,1)S(1)} %get-tuple-element.358), channel_id=1, source_target_pairs={{0,4},{4,0},{8,12},{12,8},{16,20},{20,16},{24,28},{28,24},{1,5},{5... | collective-permute-start | bytes 860168 | tf_op jit(solution)/shard_map/cond/branch_1_fun/ppermute | solution.py:209
  35.6 23.7 %collective-permute-start.37 = (bf16[6,256,128]{2,1,0:T(8,128)(2,1)S(1)}, bf16[6,256,128]{2,1,0:T(8,128)(2,1)S(1)}, u32[]{:S(2)}, u32[]{:S(2)}) collective-permute-start(bf16[6,256,128]{2,1,0:T(8,128)(2,1)S(1)} %slice.13.u_ref), channel_id=1, source_target_pairs={{0,8},{4,12},{8,0},{12,4},{16,24},{20,28},{24,16},{28,20},{1,9},{5... | collective-permute-start | bytes 1179656 | tf_op jit(solution)/shard_map/cond/branch_1_fun/ppermute | solution.py:206
  35.7 20.2 %collective-permute-start.38 = (bf16[6,256,128]{2,1,0:T(8,128)(2,1)S(1)}, bf16[6,256,128]{2,1,0:T(8,128)(2,1)S(1)}, u32[]{:S(2)}, u32[]{:S(2)}) collective-permute-start(bf16[6,256,128]{2,1,0:T(8,128)(2,1)S(1)} %slice.13.u_ref), channel_id=1, source_target_pairs={{0,16},{4,20},{8,24},{12,28},{16,0},{20,4},{24,8},{28,12},{1,17},{... | collective-permute-start | bytes 1179656 | tf_op jit(solution)/shard_map/cond/branch_1_fun/ppermute | solution.py:206
  41.3 22.5 %collective-permute-start.36 = (bf16[6,256,128]{2,1,0:T(8,128)(2,1)S(1)}, bf16[6,256,128]{2,1,0:T(8,128)(2,1)S(1)}, u32[]{:S(2)}, u32[]{:S(2)}) collective-permute-start(bf16[6,256,128]{2,1,0:T(8,128)(2,1)S(1)} %slice.13.u_ref), channel_id=1, source_target_pairs={{0,4},{4,0},{8,12},{12,8},{16,20},{20,16},{24,28},{28,24},{1,5},{5... | collective-permute-start | bytes 1179656 | tf_op jit(solution)/shard_map/cond/branch_1_fun/ppermute | solution.py:209
  42.6 6.6 %collective-permute-start.33 = (bf16[5,2,112,128]{3,2,1,0:T(8,128)(2,1)S(1)}, bf16[5,2,112,128]{3,2,1,0:T(8,128)(2,1)S(1)}, u32[]{:S(2)}, u32[]{:S(2)}) collective-permute-start(bf16[5,2,112,128]{3,2,1,0:T(8,128)(2,1)S(1)} %get-tuple-element.915), channel_id=1, source_target_pairs={{0,2},{1,3},{2,0},{3,1},{4,6},{5,7},{6,4},{7,5},{8,10},{9,11},{10,... | collective-permute-start | bytes 860168 | tf_op jit(solution)/shard_map/cond/branch_1_fun/while/body/ppermute | solution.py:219
  49.3 2.0 %collective-permute-start.34 = (bf16[10,2,112,128]{3,2,1,0:T(8,128)(2,1)S(1)}, bf16[10,2,112,128]{3,2,1,0:T(8,128)(2,1)S(1)}, u32[]{:S(2)}, u32[]{:S(2)}) collective-permute-start(bf16[10,2,112,128]{3,2,1,0:T(8,128)(2,1)S(1)} %get-tuple-element.927), channel_id=1, source_target_pairs={{0,1},{1,0},{2,3},{3,2},{4,5},{5,4},{6,7},{7,6},{8,9},{9,8},{10,11... | collective-permute-start | bytes 1720328 | tf_op jit(solution)/shard_map/cond/branch_1_fun/while/body/ppermute | solution.py:219
  51.4 6.6 %copy-start.7 = (s32[10,20]{1,0:T(8,128)S(1)}, s32[10,20]{1,0:T(8,128)}, u32[]{:S(2)}) copy-start(s32[10,20]{1,0:T(8,128)} %copy-done.6) | copy-start | bytes 2404 | tf_op jit(solution)/shard_map/cond
  51.4 6.6 %copy-start.9 = (pred[10,20]{1,0:T(8,128)(4,1)S(1)}, pred[10,20]{1,0:T(8,128)(4,1)}, u32[]{:S(2)}) copy-start(pred[10,20]{1,0:T(8,128)(4,1)} %copy-done.8) | copy-start | bytes 604 | tf_op jit(solution)/shard_map/cond
  51.4 6.7 %copy-start.11 = (s32[10]{0:T(128)S(1)}, s32[10]{0:T(128)}, u32[]{:S(2)}) copy-start(s32[10]{0:T(128)} %copy-done.10) | copy-start | bytes 124 | tf_op jit(solution)/shard_map/cond
  51.4 6.7 %copy-start.15 = (s32[10]{0:T(128)S(1)}, s32[10]{0:T(128)}, u32[]{:S(2)}) copy-start(s32[10]{0:T(128)} %copy-done.14) | copy-start | bytes 124 | tf_op jit(solution)/shard_map/cond
  55.8 10.6 %collective-permute-start.40 = (bf16[6,256,128]{2,1,0:T(8,128)(2,1)S(1)}, bf16[6,256,128]{2,1,0:T(8,128)(2,1)S(1)}, u32[]{:S(2)}, u32[]{:S(2)}) collective-permute-start(bf16[6,256,128]{2,1,0:T(8,128)(2,1)S(1)} %slice.13.u_ref), channel_id=1, source_target_pairs={{8,16},{12,20},{16,8},{20,12},{9,17},{13,21},{17,9},{21,13},{10,18... | collective-permute-start | bytes 1179656 | tf_op jit(solution)/shard_map/cond/branch_1_fun/ppermute | solution.py:206
  56.5 10.4 %collective-permute-start.41 = (bf16[6,256,128]{2,1,0:T(8,128)(2,1)S(1)}, bf16[6,256,128]{2,1,0:T(8,128)(2,1)S(1)}, u32[]{:S(2)}, u32[]{:S(2)}) collective-permute-start(bf16[6,256,128]{2,1,0:T(8,128)(2,1)S(1)} %collective-permute-done.38.refs_0_), channel_id=1, source_target_pairs={{8,0},{12,4},{16,24},{20,28},{9,1},{13,5},{17,25},{21,29},{10,2},{... | collective-permute-start | bytes 1179656 | tf_op jit(solution)/shard_map/cond/branch_1_fun/ppermute | solution.py:206
  60.5 5.9 %collective-permute-start.39 = (bf16[104,1024]{1,0:T(8,128)(2,1)S(1)}, bf16[104,1024]{1,0:T(8,128)(2,1)S(1)}, u32[]{:S(2)}, u32[]{:S(2)}) collective-permute-start(bf16[104,1024]{1,0:T(8,128)(2,1)S(1)} %get-tuple-element.368), channel_id=1, source_target_pairs={{0,4},{4,0},{8,12},{12,8},{16,20},{20,16},{24,28},{28,24},{1,5},{5... | collective-permute-start | bytes 638984 | tf_op jit(solution)/shard_map/cond/branch_1_fun/ppermute | solution.py:209
  62.2 7.8 %collective-permute-start.42 = (bf16[104,1024]{1,0:T(8,128)(2,1)S(1)}, bf16[104,1024]{1,0:T(8,128)(2,1)S(1)}, u32[]{:S(2)}, u32[]{:S(2)}) collective-permute-start(bf16[104,1024]{1,0:T(8,128)(2,1)S(1)} %get-tuple-element.373), channel_id=1, source_target_pairs={{0,4},{4,0},{8,12},{12,8},{16,20},{20,16},{24,28},{28,24},{1,5},{5... | collective-permute-start | bytes 638984 | tf_op jit(solution)/shard_map/cond/branch_1_fun/ppermute | solution.py:209
  68.1 5.9 %collective-permute-start.43 = (bf16[104,1024]{1,0:T(8,128)(2,1)S(1)}, bf16[104,1024]{1,0:T(8,128)(2,1)S(1)}, u32[]{:S(2)}, u32[]{:S(2)}) collective-permute-start(bf16[104,1024]{1,0:T(8,128)(2,1)S(1)} %get-tuple-element.374), channel_id=1, source_target_pairs={{0,4},{4,0},{8,12},{12,8},{16,20},{20,16},{24,28},{28,24},{1,5},{5... | collective-permute-start | bytes 638984 | tf_op jit(solution)/shard_map/cond/branch_1_fun/ppermute | solution.py:209
  (4 other events, 7.8 us)

commit v3 on v2

--- a/solution.py
+++ b/solution.py
@@ -81,7 +81,8 @@
     store(offset // width + 1, jnp.where(lane < shift, turned, 0.0))
 
 
-def squeeze_body(offset_ref, used_ref, u_ref, out_ref, acc):
+def squeeze_body(offset_ref, used_ref, u_ref, *refs):
+    *out_refs, acc = refs
     acc[...] = jnp.zeros_like(acc)
     for slot in range(u_ref.shape[0]):
         value = u_ref[slot].astype(jnp.float32)
@@ -91,7 +92,9 @@
             acc[tile] += part
 
         place_columns(jnp.where(lane < used_ref[slot], value, 0.0), offset_ref[slot], store)
-    out_ref[...] = acc[: out_ref.shape[0]].astype(out_ref.dtype)
+    packed = acc[...].astype(u_ref.dtype)
+    for out_ref in out_refs:
+        out_ref[...] = packed[: out_ref.shape[0]]
 
 
 def land_body(index_ref, target_ref, offset_ref, comp_ref, rows_ref):
@@ -251,7 +254,7 @@
     level = sum((fullest > count * rank_max).astype(jnp.int32) for count in tiles[:-1])
     squeezed = call(
         squeeze_body,
-        jax.ShapeDtypeStruct(u_factors.shape, u_factors.dtype),
+        [jax.ShapeDtypeStruct((count, seg, rank_max), u_factors.dtype) for count in tiles],
         [SMEM, SMEM, VMEM],
         "squeeze",
         moved=4 * u_factors.size,
@@ -266,7 +269,7 @@
     )
 
     def rest(count, x_low, x_high, v_near, v_far, v_middle, v_ends, squeezed):
-        target_factors = squeezed[:count]
+        target_factors = squeezed[tiles.index(count)]
         u_far, u_near = move(target_factors, far), move(target_factors, near)
         partial, sent = call(
             functools.partial(compress_body, seg),
@@ -298,8 +301,6 @@
                 0, rounds, lambda _, array, stage=stage: swapped(array, stage), gathered
             )
             gathered = jnp.concatenate([gathered, other], axis=0)
-        u_ends = move(after(u_far, gathered), ends)
-        u_middle = move(after(target_factors, u_far, gathered), middle)
         slot_rows = call(
             land_body,
             jax.ShapeDtypeStruct((count, clusters, 2 * padded, rank_max), jnp.bfloat16),
@@ -321,7 +322,12 @@
             scratch=[pltpu.VMEM((clusters, padded, seg), jnp.float32)],
         )(position, slot_rows, target_factors, u_side)
         finished = []
-        for step, shards in ((1, [u_near]), (2, [u_far]), (3, [u_middle, u_ends])):
+        for step in range(1, PLACES):
+            if step == 2:
+                u_far = after(u_far, own_parts[1])
+                u_ends = move(u_far, ends)
+                u_middle = move(after(target_factors, u_far), middle)
+            shards = [u_near] if step == 1 else [u_far] if step == 2 else [u_middle, u_ends]
             if finished:
                 slot_rows = after(slot_rows, own_parts[finished[-1]])
             if len(finished) == 2:

time: 77.6 us -> 88 us (1.13)
  other arithmetic: 1.88 us -> 7.77 us
  waiting for transfers between devices: 32.5 us -> 37.3 us
  Pallas kernels: 11.8 us -> 14.2 us
    ppermute x8, waiting for transfers between devices: 7.58 us -> 18.1 us  [move(): lax.ppermute(array, 'rhs', [(2 * a + i, 2 * b + i) for a, b in pairs for...]
    ppermute x7, waiting for transfers between devices: 14.7 us -> 11.5 us  [across(): return lax.ppermute(array, 'rhs', [(p, p ^ 1) for p in range(2 * PLACES)])]
    ppermute x4, waiting for transfers between devices: 10.2 us -> 7.64 us  [swapped(): return lax.ppermute(array, 'clus', [(p, p ^ stage) for p in range(owners)])]
    pallas_call x1, Pallas kernels: 1.04 us -> 2.48 us  [paired(): call(squeeze_body, [jax.ShapeDtypeStruct((count, seg, rank_max), u_factor...]
    concatenate x2, other arithmetic: 0.15 us -> 1.42 us  [double(): return jnp.concatenate([array, swapped(array, stage)], axis=0)]
    another operation x1, other arithmetic: 0.01 us -> 1.24 us  [paired(): table = jnp.stack([block_slot, block_rank], axis=1)]
    pallas_call x1, Pallas kernels: 0.7 us -> 1.89 us  [rest(): call(functools.partial(join_body, seg, clusters), jax.ShapeDtypeStruct((c...]
    unnamed x14 -> x12, local copies, waits for them, and re-layouts: 1.2 us -> 0.02 us
  transfers between devices with their start and end apart: 19 -> 19, of which waited for: 13 -> 9; matrix products, arithmetic and copies ran while one was open for 3% -> 9% of each run, Pallas kernels for 11% -> 11%
where the time goes in v3:
time: 88 us; the launch traced here: 87 us
  waiting for transfers between devices  37.3 us (42%)
  starting transfers between devices  24.5 us (28%)
  Pallas kernels  14.2 us (16%)
  other arithmetic  7.77 us (9%)
  between operations  2.39 us (3%)
    ppermute x8, waiting for transfers between devices, move(): lax.ppermute(array, 'rhs', [(2 * a + i, 2 * b + i) for a, b in pairs for...  18.1 us
    ppermute x8, starting transfers between devices, move(): lax.ppermute(array, 'rhs', [(2 * a + i, 2 * b + i) for a, b in pairs for...  13.4 us
    ppermute x7, waiting for transfers between devices, across(): return lax.ppermute(array, 'rhs', [(p, p ^ 1) for p in range(2 * PLACES)])  11.5 us
    ppermute x7, starting transfers between devices, across(): return lax.ppermute(array, 'rhs', [(p, p ^ 1) for p in range(2 * PLACES)])  7.96 us
    ppermute x4, waiting for transfers between devices, swapped(): return lax.ppermute(array, 'clus', [(p, p ^ stage) for p in range(owners)])  7.64 us
    pallas_call x3, Pallas kernels, rest(): call(functools.partial(expand_body, seg, columns), [chunk, chunk], [SMEM,...  3.46 us
    ppermute x4, starting transfers between devices, swapped(): return lax.ppermute(array, 'clus', [(p, p ^ stage) for p in range(owners)])  3.11 us
    pallas_call x1, Pallas kernels, paired(): call(squeeze_body, [jax.ShapeDtypeStruct((count, seg, rank_max), u_factor...  2.48 us
  transfers between devices with their start and end apart: 19, of which 9 were waited for; matrix products, arithmetic and copies ran while one was open for 9% of the time, Pallas kernels for 11%

profile of v3, /device:TPU:0, one launch (start us, length us, event | category | flops | bytes accessed | tf_op | source)
XLA Modules:
  0.0 87.0 jit_solution(15794014158732797449)
XLA Ops:
  0.8 5.8 %collective-permute-start.58 = (bf16[5,256,128]{2,1,0:T(8,128)(2,1)}, bf16[5,256,128]{2,1,0:T(8,128)(2,1)}, u32[]{:S(2)}, u32[]{:S(2)}) collective-permute-start(bf16[5,256,128]{2,1,0:T(8,128)(2,1)} %param.33), channel_id=1, source_target_pairs={{0,16},{4,20},{8,24},{12,28},{16,0},{20,4},{24,8},{28,12},{1,17},{... | collective-permute-start | bytes 983048 | tf_op jit(solution)/shard_map/ppermute | solution.py:209
  6.8 1.2 %pad_add_fusion = s32[5,2]{0,1:T(2,128)} fusion(s32[5,1]{0,1:T(1,128)} %bitcast.11, s32[5,1]{0,1:T(1,128)} %bitcast.8), kind=kLoop, calls=%fused_computation.27 | loop fusion | flops 10 | bytes 80 | tf_op jit(solution)/shard_map/stack | solution.py:238
  8.0 1.5 %collective-permute-start.61 = (s32[5,2]{0,1:T(2,128)}, s32[5,2]{0,1:T(2,128)}, u32[]{:S(2)}, u32[]{:S(2)}) collective-permute-start(s32[5,2]{0,1:T(2,128)} %pad_add_fusion), channel_id=1, source_target_pairs={{0,2},{1,3},{2,0},{3,1},{4,6},{5,7},{6,4},{7,5},{8,10},{9,11},{10,... | collective-permute-start | bytes 128 | tf_op jit(solution)/shard_map/ppermute | solution.py:222
  9.6 1.7 %pack.1 = (bf16[104,2048]{1,0:T(8,128)(2,1)S(1)}, bf16[104,2048]{1,0:T(8,128)(2,1)S(1)}) custom-call(s32[2]{0:T(128)S(1)} %pad_add_fusion.3.pos_ref, bf16[104,8192]{1,0:T(8,128)(2,1)} %x_ref.1), custom_call_target="tpu_custom_call" | custom-call | bytes 2555904 | tf_op jit(solution)/shard_map/pack/pallas_call | solution.py:228
  11.4 1.6 %collective-permute-start.55 = (bf16[104,2048]{1,0:T(8,128)(2,1)S(1)}, bf16[104,2048]{1,0:T(8,128)(2,1)}, u32[]{:S(2)}, u32[]{:S(2)}) collective-permute-start(bf16[104,2048]{1,0:T(8,128)(2,1)S(1)} %get-tuple-element.521), channel_id=1, source_target_pairs={{0,4},{4,0},{8,12},{12,8},{16,20},{20,16},{24,28},{28,24},{1,5},{5... | collective-permute-start | bytes 1277960 | tf_op jit(solution)/shard_map/ppermute | solution.py:212
  16.6 11.8 %collective-permute-done.58 = bf16[5,256,128]{2,1,0:T(8,128)(2,1)} collective-permute-done((bf16[5,256,128]{2,1,0:T(8,128)(2,1)}, bf16[5,256,128]{2,1,0:T(8,128)(2,1)}, u32[]{:S(2)}, u32[]{:S(2)}) %collective-permute-start.58) | collective-permute-done | bytes 327712 | tf_op jit(solution)/shard_map/ppermute | solution.py:209
  28.3 1.3 %collective-permute-start.60 = (bf16[5,256,128]{2,1,0:T(8,128)(2,1)}, bf16[5,256,128]{2,1,0:T(8,128)(2,1)}, u32[]{:S(2)}, u32[]{:S(2)}) collective-permute-start(bf16[5,256,128]{2,1,0:T(8,128)(2,1)} %collective-permute-done.58), channel_id=1, source_target_pairs={{8,0},{12,4},{16,24},{20,28},{9,1},{13,5},{17,25},{21,29},{10,2},{... | collective-permute-start | bytes 983048 | tf_op jit(solution)/shard_map/ppermute | solution.py:209
  29.6 1.3 %select_reduce_fusion.1 = s32[4]{0:T(128)} fusion(s32[20]{0:T(128)S(1)} %get-tuple-element.604, s32[20]{0:T(128)S(1)} %get-tuple-element.605, s32[4]{0:T(128)} %get-tuple-element.606, s32[4]{0:T(128)} %get-tuple-element.607), kind=kLoop, calls=%fused_computation.26 | loop fusion | flops 396 | bytes 208 | tf_op jit(solution)/shard_map/reduce_sum | solution.py:252
  30.9 1.3 %reduce_max.18 = s32[]{:T(128)} reduce(s32[4]{0:T(128)} %select_reduce_fusion.1, s32[]{:T(128)} %constant.95.clone.1), dimensions={0}, to_apply=%region_3.4 | reduce | flops 3 | bytes 24 | tf_op jit(solution)/shard_map/reduce_max | solution.py:252
  35.5 2.5 %squeeze.1 = (bf16[5,256,128]{2,1,0:T(8,128)(2,1)}, bf16[6,256,128]{2,1,0:T(8,128)(2,1)}, bf16[7,256,128]{2,1,0:T(8,128)(2,1)}, bf16[8,256,128]{2,1,0:T(8,128)(2,1)}, bf16[10,256,128]{2,1,0:T(8,128)(2,1)}) custom-call(s32[10]{0:T(128)S(1)} %select_reduce_fusion.offset_ref, s32[10]{0:T(128)S(1)} %get-tuple-element.543.used_ref, bf16[10,256,128]{2,1,0:T(8,128)(2,1)S(1)} %copy-done), custom_call_target="tpu_custom_call" | custom-call | bytes 1310720 | tf_op jit(solution)/shard_map/squeeze/pallas_call | solution.py:255
  39.1 47.9 %conditional.1 = (bf16[104,8192]{1,0:T(8,128)(2,1)}) conditional(s32[]{:T(128)} %clamp.3, (s32[5]{0:T(128)}, s32[2]{0:T(128)S(1)}, s32[5]{0:T(128)S(1)}, bf16[104,8192]{1,0:T(8,128)(2,1)S(1)}, bf16[104,2048]{1,0:T(8,128)(2,1)}, /*index=5*/bf16[104,2048]{1,0:T(8,128)(2,1)}, bf16[5,256,128]{2,1,0:T(8,128)(2,1)}, ...), branch_computations={%region_5.10_spmd, %region_10.15_spmd, %region_15.20_spmd, %region... | conditional | flops 2455675392 | bytes 61114600 | solution.py:354
  39.1 2.5 %compress.5 = (f32[5,2,112,128]{3,2,1,0:T(8,128)S(1)}, bf16[5,2,112,128]{3,2,1,0:T(8,128)(2,1)S(1)}) custom-call(s32[2]{0:T(128)S(1)} %get-tuple-element.301.pos_ref, s32[5]{0:T(128)S(1)} %get-tuple-element.306.source_ref, bf16[104,8192]{1,0:T(8,128)(2,1)S(1)} %get-tuple-element.307.x_ref, bf16[104,2048]{1,0:T(8,128)(2,1)} %get-tuple-element.308.xl_ref, ...), custom_call_target="tpu_custom_call" | custom-call | flops 272629760 | bytes 3866624 | tf_op jit(solution)/shard_map/cond/branch_0_fun/compress/pallas_call | solution.py:274
  41.6 1.6 %collective-permute-start.46 = (bf16[5,2,112,128]{3,2,1,0:T(8,128)(2,1)S(1)}, bf16[5,2,112,128]{3,2,1,0:T(8,128)(2,1)S(1)}, u32[]{:S(2)}, u32[]{:S(2)}) collective-permute-start(bf16[5,2,112,128]{3,2,1,0:T(8,128)(2,1)S(1)} %get-tuple-element.316), channel_id=1, source_target_pairs={{0,4},{4,0},{8,12},{12,8},{16,20},{20,16},{24,28},{28,24},{1,5},{5... | collective-permute-start | bytes 860168 | tf_op jit(solution)/shard_map/cond/branch_0_fun/ppermute | solution.py:212
  43.1 3.4 %collective-permute-start.49 = (bf16[5,256,128]{2,1,0:T(8,128)(2,1)S(1)}, bf16[5,256,128]{2,1,0:T(8,128)(2,1)S(1)}, u32[]{:S(2)}, u32[]{:S(2)}) collective-permute-start(bf16[5,256,128]{2,1,0:T(8,128)(2,1)S(1)} %copy-done.5), channel_id=1, source_target_pairs={{0,16},{4,20},{8,24},{12,28},{16,0},{20,4},{24,8},{28,12},{1,17},{... | collective-permute-start | bytes 983048 | tf_op jit(solution)/shard_map/cond/branch_0_fun/ppermute | solution.py:209
  46.6 1.9 %collective-permute-done.46 = bf16[5,2,112,128]{3,2,1,0:T(8,128)(2,1)S(1)} collective-permute-done((bf16[5,2,112,128]{3,2,1,0:T(8,128)(2,1)S(1)}, bf16[5,2,112,128]{3,2,1,0:T(8,128)(2,1)S(1)}, u32[]{:S(2)}, u32[]{:S(2)}) %collective-permute-start.46) | collective-permute-done | bytes 286752 | tf_op jit(solution)/shard_map/cond/branch_0_fun/ppermute | solution.py:212
  48.6 1.6 %collective-permute-start.47 = (bf16[5,256,128]{2,1,0:T(8,128)(2,1)S(1)}, bf16[5,256,128]{2,1,0:T(8,128)(2,1)S(1)}, u32[]{:S(2)}, u32[]{:S(2)}) collective-permute-start(bf16[5,256,128]{2,1,0:T(8,128)(2,1)S(1)} %copy-done.5), channel_id=1, source_target_pairs={{0,4},{4,0},{8,12},{12,8},{16,20},{20,16},{24,28},{28,24},{1,5},{5... | collective-permute-start | bytes 983048 | tf_op jit(solution)/shard_map/cond/branch_0_fun/ppermute | solution.py:212
  50.1 6.7 %while.90 = (s32[]{:T(128)}, bf16[5,2,112,128]{3,2,1,0:T(8,128)(2,1)S(1)}, s32[]{:T(128)}, s32[]{:T(128)}) while((s32[]{:T(128)}, bf16[5,2,112,128]{3,2,1,0:T(8,128)(2,1)S(1)}, s32[]{:T(128)}, s32[]{:T(128)}) %tuple.211), condition=%wide.region_7.7_spmd, body=%wide.region_6.6_spmd.sunk | while | flops 2 | bytes 1720413 | solution.py:300
  50.1 1.5 %collective-permute-start.44 = (bf16[5,2,112,128]{3,2,1,0:T(8,128)(2,1)S(1)}, bf16[5,2,112,128]{3,2,1,0:T(8,128)(2,1)S(1)}, u32[]{:S(2)}, u32[]{:S(2)}) collective-permute-start(bf16[5,2,112,128]{3,2,1,0:T(8,128)(2,1)S(1)} %get-tuple-element.909), channel_id=1, source_target_pairs={{0,2},{1,3},{2,0},{3,1},{4,6},{5,7},{6,4},{7,5},{8,10},{9,11},{10,... | collective-permute-start | bytes 860168 | tf_op jit(solution)/shard_map/cond/branch_0_fun/while/body/ppermute | solution.py:222
  51.7 5.1 %collective-permute-done.44 = bf16[5,2,112,128]{3,2,1,0:T(8,128)(2,1)S(1)} collective-permute-done((bf16[5,2,112,128]{3,2,1,0:T(8,128)(2,1)S(1)}, bf16[5,2,112,128]{3,2,1,0:T(8,128)(2,1)S(1)}, u32[]{:S(2)}, u32[]{:S(2)}) %collective-permute-start.44) | collective-permute-done | bytes 286752 | tf_op jit(solution)/shard_map/cond/branch_0_fun/while/body/ppermute | solution.py:222
  56.9 2.1 %while.91 = (s32[]{:T(128)}, bf16[10,2,112,128]{3,2,1,0:T(8,128)(2,1)S(1)}, s32[]{:T(128)}, s32[]{:T(128)}) while((s32[]{:T(128)}, bf16[10,2,112,128]{3,2,1,0:T(8,128)(2,1)S(1)}, s32[]{:T(128)}, s32[]{:T(128)}) %tuple.214), condition=%wide.region_9.9_spmd, body=%wide.region_8.8_spmd.sunk | while | flops 2 | bytes 3440733 | solution.py:300
  57.0 2.0 %collective-permute-done.45 = bf16[10,2,112,128]{3,2,1,0:T(8,128)(2,1)S(1)} collective-permute-done((bf16[10,2,112,128]{3,2,1,0:T(8,128)(2,1)S(1)}, bf16[10,2,112,128]{3,2,1,0:T(8,128)(2,1)S(1)}, u32[]{:S(2)}, u32[]{:S(2)}) %collective-permute-start.45) | collective-permute-done | bytes 573472 | tf_op jit(solution)/shard_map/cond/branch_0_fun/while/body/ppermute | solution.py:222
  59.6 1.1 %land.5.rows_ref = bf16[5,4,224,128]{3,2,1,0:T(8,128)(2,1)S(1)} custom-call(s32[10]{0:T(128)S(1)} %get-tuple-element.302.index_ref, s32[10]{0:T(128)S(1)} %copy-done.7, s32[10]{0:T(128)S(1)} %get-tuple-element.304.offset_ref, bf16[20,2,112,128]{3,2,1,0:T(8,128)(2,1)S(1)} %pad_maximum_fusion.comp_ref), custom_call_target="tpu_custom_call" | custom-call | bytes 5734400 | tf_op jit(solution)/shard_map/cond/branch_0_fun/land/pallas_call | solution.py:304
  60.8 1.1 %expand.15 = (bf16[104,1024]{1,0:T(8,128)(2,1)S(1)}, bf16[104,1024]{1,0:T(8,128)(2,1)S(1)}) custom-call(s32[2]{0:T(128)S(1)} %get-tuple-element.301.pos_ref, bf16[5,4,224,128]{3,2,1,0:T(8,128)(2,1)S(1)} %land.5.rows_ref, bf16[5,256,128]{2,1,0:T(8,128)(2,1)S(1)} %collective-permute-done.48.refs_0_), custom_call_target="tpu_custom_call" | custom-call | flops 272629760 | bytes 1900544 | tf_op jit(solution)/shard_map/cond/branch_0_fun/expand/pallas_call | solution.py:335
  62.6 1.3 %collective-permute-start.52 = (bf16[5,256,128]{2,1,0:T(8,128)(2,1)S(1)}, bf16[5,256,128]{2,1,0:T(8,128)(2,1)S(1)}, u32[]{:S(2)}, u32[]{:S(2)}) collective-permute-start(bf16[5,256,128]{2,1,0:T(8,128)(2,1)S(1)} %collective-permute-done.49.refs_0_), channel_id=1, source_target_pairs={{8,0},{12,4},{16,24},{20,28},{9,1},{13,5},{17,25},{21,29},{10,2},{... | collective-permute-start | bytes 983048 | tf_op jit(solution)/shard_map/cond/branch_0_fun/ppermute | solution.py:209
  64.5 1.1 %expand.16 = (bf16[104,1024]{1,0:T(8,128)(2,1)S(1)}, bf16[104,1024]{1,0:T(8,128)(2,1)S(1)}) custom-call(s32[2]{0:T(128)S(1)} %get-tuple-element.301.pos_ref, bf16[5,4,224,128]{3,2,1,0:T(8,128)(2,1)S(1)} %land.5.rows_ref, bf16[5,256,128]{2,1,0:T(8,128)(2,1)S(1)} %collective-permute-done.49.refs_0_), custom_call_target="tpu_custom_call" | custom-call | flops 272629760 | bytes 1900544 | tf_op jit(solution)/shard_map/cond/branch_0_fun/expand/pallas_call | solution.py:335
  65.7 1.5 %collective-permute-start.53 = (bf16[104,1024]{1,0:T(8,128)(2,1)S(1)}, bf16[104,1024]{1,0:T(8,128)(2,1)S(1)}, u32[]{:S(2)}, u32[]{:S(2)}) collective-permute-start(bf16[104,1024]{1,0:T(8,128)(2,1)S(1)} %get-tuple-element.331), channel_id=1, source_target_pairs={{0,4},{4,0},{8,12},{12,8},{16,20},{20,16},{24,28},{28,24},{1,5},{5... | collective-permute-start | bytes 638984 | tf_op jit(solution)/shard_map/cond/branch_0_fun/ppermute | solution.py:212
  67.2 1.1 %expand_own.5.first_ref = bf16[104,2048]{1,0:T(8,128)(2,1)S(1)} custom-call(s32[2]{0:T(128)S(1)} %get-tuple-element.301.pos_ref, bf16[5,4,224,128]{3,2,1,0:T(8,128)(2,1)S(1)} %land.5.rows_ref, bf16[5,256,128]{2,1,0:T(8,128)(2,1)S(1)} %copy-done.5, bf16[5,256,128]{2,1,0:T(8,128)(2,1)S(1)} %collective-permute-done.47.side_ref), custom_call_target="tpu_custom_call" | custom-call | flops 272629760 | bytes 2228224 | tf_op jit(solution)/shard_map/cond/branch_0_fun/expand_own/pallas_call | solution.py:315
  68.4 3.7 %collective-permute-done.50.refs_3_ = bf16[104,1024]{1,0:T(8,128)(2,1)S(1)} collective-permute-done((bf16[104,1024]{1,0:T(8,128)(2,1)S(1)}, bf16[104,1024]{1,0:T(8,128)(2,1)S(1)}, u32[]{:S(2)}, u32[]{:S(2)}) %collective-permute-start.50) | collective-permute-done | bytes 213024 | tf_op jit(solution)/shard_map/cond/branch_0_fun/ppermute | solution.py:212
  72.1 5.3 %collective-permute-done.52.refs_1_ = bf16[5,256,128]{2,1,0:T(8,128)(2,1)S(1)} collective-permute-done((bf16[5,256,128]{2,1,0:T(8,128)(2,1)S(1)}, bf16[5,256,128]{2,1,0:T(8,128)(2,1)S(1)}, u32[]{:S(2)}, u32[]{:S(2)}) %collective-permute-start.52) | collective-permute-done | bytes 327712 | tf_op jit(solution)/shard_map/cond/branch_0_fun/ppermute | solution.py:209
  77.4 1.2 %expand.17 = (bf16[104,1024]{1,0:T(8,128)(2,1)S(1)}, bf16[104,1024]{1,0:T(8,128)(2,1)S(1)}) custom-call(s32[2]{0:T(128)S(1)} %get-tuple-element.301.pos_ref, bf16[5,4,224,128]{3,2,1,0:T(8,128)(2,1)S(1)} %land.5.rows_ref, bf16[5,256,128]{2,1,0:T(8,128)(2,1)S(1)} %collective-permute-done.51.refs_0_, bf16[5,256,128]{2,1,0:T(8,128)(2,1)S(1)} %collective-permute-done.52.refs_1_), custom_call_target="tpu_custom_call" | custom-call | flops 272629760 | bytes 1900544 | tf_op jit(solution)/shard_map/cond/branch_0_fun/expand/pallas_call | solution.py:335
  79.2 5.9 %collective-permute-done.54.refs_5_ = bf16[104,1024]{1,0:T(8,128)(2,1)S(1)} collective-permute-done((bf16[104,1024]{1,0:T(8,128)(2,1)S(1)}, bf16[104,1024]{1,0:T(8,128)(2,1)S(1)}, u32[]{:S(2)}, u32[]{:S(2)}) %collective-permute-start.54) | collective-permute-done | bytes 213024 | tf_op jit(solution)/shard_map/cond/branch_0_fun/ppermute | solution.py:212
  85.1 1.9 %join.5 = bf16[104,8192]{1,0:T(8,128)(2,1)} custom-call(s32[2]{0:T(128)S(1)} %get-tuple-element.301.pos_ref, bf16[104,2048]{1,0:T(8,128)(2,1)S(1)} %expand_own.5.first_ref, bf16[104,1024]{1,0:T(8,128)(2,1)S(1)} %get-tuple-element.322.refs_0_, bf16[104,1024]{1,0:T(8,128)(2,1)S(1)} %get-tuple-element.325.refs_1_, ...), custom_call_target="tpu_custom_call" | custom-call | bytes 3407872 | tf_op jit(solution)/shard_map/cond/branch_0_fun/join/pallas_call | solution.py:346
  (54 shorter events, 9.7 us)
Async XLA Ops:
  0.0 13.4 %copy-start.14 = (s32[5]{0:T(128)S(1)}, s32[5]{0:T(128)}, u32[]{:S(2)}) copy-start(s32[5]{0:T(128)} %param.36) | copy-start | bytes 64
  0.0 13.4 %copy-start.13 = (s32[5]{0:T(128)S(1)}, s32[5]{0:T(128)}, u32[]{:S(2)}) copy-start(s32[5]{0:T(128)} %param.37) | copy-start | bytes 64
  0.0 35.5 %copy-start = (bf16[10,256,128]{2,1,0:T(8,128)(2,1)S(1)}, bf16[10,256,128]{2,1,0:T(8,128)(2,1)}, u32[]{:S(2)}) copy-start(bf16[10,256,128]{2,1,0:T(8,128)(2,1)} %u_ref.1) | copy-start | bytes 1966084
  0.0 38.0 %collective-permute-start.59 = (bf16[5,256,128]{2,1,0:T(8,128)(2,1)}, bf16[5,256,128]{2,1,0:T(8,128)(2,1)S(1)}, u32[]{:S(2)}, u32[]{:S(2)}) collective-permute-start(bf16[5,256,128]{2,1,0:T(8,128)(2,1)} %param.33), channel_id=1, source_target_pairs={{8,16},{12,20},{16,8},{20,12},{9,17},{13,21},{17,9},{21,13},{10,18... | collective-permute-start | bytes 983048 | tf_op jit(solution)/shard_map/ppermute | solution.py:209
  0.8 27.5 %collective-permute-start.58 = (bf16[5,256,128]{2,1,0:T(8,128)(2,1)}, bf16[5,256,128]{2,1,0:T(8,128)(2,1)}, u32[]{:S(2)}, u32[]{:S(2)}) collective-permute-start(bf16[5,256,128]{2,1,0:T(8,128)(2,1)} %param.33), channel_id=1, source_target_pairs={{0,16},{4,20},{8,24},{12,28},{16,0},{20,4},{24,8},{28,12},{1,17},{... | collective-permute-start | bytes 983048 | tf_op jit(solution)/shard_map/ppermute | solution.py:209
  6.6 31.4 %collective-permute-start.57 = (bf16[5,256,128]{2,1,0:T(8,128)(2,1)}, bf16[5,256,128]{2,1,0:T(8,128)(2,1)}, u32[]{:S(2)}, u32[]{:S(2)}) collective-permute-start(bf16[5,256,128]{2,1,0:T(8,128)(2,1)} %param.33), channel_id=1, source_target_pairs={{0,8},{4,12},{8,0},{12,4},{16,24},{20,28},{24,16},{28,20},{1,9},{5... | collective-permute-start | bytes 983048 | tf_op jit(solution)/shard_map/ppermute | solution.py:209
  8.0 5.4 %collective-permute-start.61 = (s32[5,2]{0,1:T(2,128)}, s32[5,2]{0,1:T(2,128)}, u32[]{:S(2)}, u32[]{:S(2)}) collective-permute-start(s32[5,2]{0,1:T(2,128)} %pad_add_fusion), channel_id=1, source_target_pairs={{0,2},{1,3},{2,0},{3,1},{4,6},{5,7},{6,4},{7,5},{8,10},{9,11},{10,... | collective-permute-start | bytes 128 | tf_op jit(solution)/shard_map/ppermute | solution.py:222
  9.6 29.4 %copy-start.1 = (bf16[104,8192]{1,0:T(8,128)(2,1)S(1)}, bf16[104,8192]{1,0:T(8,128)(2,1)}, u32[]{:S(2)}) copy-start(bf16[104,8192]{1,0:T(8,128)(2,1)} %x_ref.1) | copy-start | bytes 5111812
  9.6 29.4 %copy-start.6 = (s32[5]{0:T(128)S(1)}, s32[5]{0:T(128)}, u32[]{:S(2)}) copy-start(s32[5]{0:T(128)} %param.35) | copy-start | bytes 64
  11.4 26.7 %collective-permute-start.55 = (bf16[104,2048]{1,0:T(8,128)(2,1)S(1)}, bf16[104,2048]{1,0:T(8,128)(2,1)}, u32[]{:S(2)}, u32[]{:S(2)}) collective-permute-start(bf16[104,2048]{1,0:T(8,128)(2,1)S(1)} %get-tuple-element.521), channel_id=1, source_target_pairs={{0,4},{4,0},{8,12},{12,8},{16,20},{20,16},{24,28},{28,24},{1,5},{5... | collective-permute-start | bytes 1277960 | tf_op jit(solution)/shard_map/ppermute | solution.py:212
  14.2 1.1 %collective-permute-start.62 = (s32[10,2]{0,1:T(2,128)S(1)}, s32[10,2]{0,1:T(2,128)S(1)}, u32[]{:S(2)}, u32[]{:S(2)}) collective-permute-start(s32[10,2]{0,1:T(2,128)S(1)} %pad_add_fusion.1), channel_id=1, source_target_pairs={{0,1},{1,0},{2,3},{3,2},{4,5},{5,4},{6,7},{7,6},{8,9},{9,8},{10,11... | collective-permute-start | bytes 248 | tf_op jit(solution)/shard_map/ppermute | solution.py:222
  15.3 22.7 %collective-permute-start.56 = (bf16[104,2048]{1,0:T(8,128)(2,1)S(1)}, bf16[104,2048]{1,0:T(8,128)(2,1)}, u32[]{:S(2)}, u32[]{:S(2)}) collective-permute-start(bf16[104,2048]{1,0:T(8,128)(2,1)S(1)} %get-tuple-element.522), channel_id=1, source_target_pairs={{0,4},{4,0},{8,12},{12,8},{16,20},{20,16},{24,28},{28,24},{1,5},{5... | collective-permute-start | bytes 1277960 | tf_op jit(solution)/shard_map/ppermute | solution.py:212
  16.6 18.0 %copy-start.12 = (s32[20]{0:T(128)}, s32[20]{0:T(128)S(1)}, u32[]{:S(2)}) copy-start(s32[20]{0:T(128)S(1)} %get-tuple-element.605) | copy-start | bytes 244
  28.3 10.8 %collective-permute-start.60 = (bf16[5,256,128]{2,1,0:T(8,128)(2,1)}, bf16[5,256,128]{2,1,0:T(8,128)(2,1)}, u32[]{:S(2)}, u32[]{:S(2)}) collective-permute-start(bf16[5,256,128]{2,1,0:T(8,128)(2,1)} %collective-permute-done.58), channel_id=1, source_target_pairs={{8,0},{12,4},{16,24},{20,28},{9,1},{13,5},{17,25},{21,29},{10,2},{... | collective-permute-start | bytes 983048 | tf_op jit(solution)/shard_map/ppermute | solution.py:209
  39.1 4.0 %copy-start.5 = (bf16[5,256,128]{2,1,0:T(8,128)(2,1)S(1)}, bf16[5,256,128]{2,1,0:T(8,128)(2,1)}, u32[]{:S(2)}) copy-start(bf16[5,256,128]{2,1,0:T(8,128)(2,1)} %get-tuple-element.329.u_ref) | copy-start | bytes 983044 | tf_op jit(solution)/shard_map/cond
  39.1 7.4 %copy-start.15 = (s32[5]{0:T(128)S(1)}, s32[5]{0:T(128)}, u32[]{:S(2)}) copy-start(s32[5]{0:T(128)} %get-tuple-element.305) | copy-start | bytes 64 | tf_op jit(solution)/shard_map/cond
  41.6 6.9 %collective-permute-start.46 = (bf16[5,2,112,128]{3,2,1,0:T(8,128)(2,1)S(1)}, bf16[5,2,112,128]{3,2,1,0:T(8,128)(2,1)S(1)}, u32[]{:S(2)}, u32[]{:S(2)}) collective-permute-start(bf16[5,2,112,128]{3,2,1,0:T(8,128)(2,1)S(1)} %get-tuple-element.316), channel_id=1, source_target_pairs={{0,4},{4,0},{8,12},{12,8},{16,20},{20,16},{24,28},{28,24},{1,5},{5... | collective-permute-start | bytes 860168 | tf_op jit(solution)/shard_map/cond/branch_0_fun/ppermute | solution.py:212
  43.1 18.8 %collective-permute-start.49 = (bf16[5,256,128]{2,1,0:T(8,128)(2,1)S(1)}, bf16[5,256,128]{2,1,0:T(8,128)(2,1)S(1)}, u32[]{:S(2)}, u32[]{:S(2)}) collective-permute-start(bf16[5,256,128]{2,1,0:T(8,128)(2,1)S(1)} %copy-done.5), channel_id=1, source_target_pairs={{0,16},{4,20},{8,24},{12,28},{16,0},{20,4},{24,8},{28,12},{1,17},{... | collective-permute-start | bytes 983048 | tf_op jit(solution)/shard_map/cond/branch_0_fun/ppermute | solution.py:209
  46.5 14.2 %collective-permute-start.48 = (bf16[5,256,128]{2,1,0:T(8,128)(2,1)S(1)}, bf16[5,256,128]{2,1,0:T(8,128)(2,1)S(1)}, u32[]{:S(2)}, u32[]{:S(2)}) collective-permute-start(bf16[5,256,128]{2,1,0:T(8,128)(2,1)S(1)} %copy-done.5), channel_id=1, source_target_pairs={{0,8},{4,12},{8,0},{12,4},{16,24},{20,28},{24,16},{28,20},{1,9},{5... | collective-permute-start | bytes 983048 | tf_op jit(solution)/shard_map/cond/branch_0_fun/ppermute | solution.py:209
  48.6 18.7 %collective-permute-start.47 = (bf16[5,256,128]{2,1,0:T(8,128)(2,1)S(1)}, bf16[5,256,128]{2,1,0:T(8,128)(2,1)S(1)}, u32[]{:S(2)}, u32[]{:S(2)}) collective-permute-start(bf16[5,256,128]{2,1,0:T(8,128)(2,1)S(1)} %copy-done.5), channel_id=1, source_target_pairs={{0,4},{4,0},{8,12},{12,8},{16,20},{20,16},{24,28},{28,24},{1,5},{5... | collective-permute-start | bytes 983048 | tf_op jit(solution)/shard_map/cond/branch_0_fun/ppermute | solution.py:212
  50.1 6.6 %collective-permute-start.44 = (bf16[5,2,112,128]{3,2,1,0:T(8,128)(2,1)S(1)}, bf16[5,2,112,128]{3,2,1,0:T(8,128)(2,1)S(1)}, u32[]{:S(2)}, u32[]{:S(2)}) collective-permute-start(bf16[5,2,112,128]{3,2,1,0:T(8,128)(2,1)S(1)} %get-tuple-element.909), channel_id=1, source_target_pairs={{0,2},{1,3},{2,0},{3,1},{4,6},{5,7},{6,4},{7,5},{8,10},{9,11},{10,... | collective-permute-start | bytes 860168 | tf_op jit(solution)/shard_map/cond/branch_0_fun/while/body/ppermute | solution.py:222
  56.9 2.0 %collective-permute-start.45 = (bf16[10,2,112,128]{3,2,1,0:T(8,128)(2,1)S(1)}, bf16[10,2,112,128]{3,2,1,0:T(8,128)(2,1)S(1)}, u32[]{:S(2)}, u32[]{:S(2)}) collective-permute-start(bf16[10,2,112,128]{3,2,1,0:T(8,128)(2,1)S(1)} %get-tuple-element.921), channel_id=1, source_target_pairs={{0,1},{1,0},{2,3},{3,2},{4,5},{5,4},{6,7},{7,6},{8,9},{9,8},{10,11... | collective-permute-start | bytes 1720328 | tf_op jit(solution)/shard_map/cond/branch_0_fun/while/body/ppermute | solution.py:222
  59.0 0.7 copy-start.7
  61.9 10.2 %collective-permute-start.51 = (bf16[5,256,128]{2,1,0:T(8,128)(2,1)S(1)}, bf16[5,256,128]{2,1,0:T(8,128)(2,1)S(1)}, u32[]{:S(2)}, u32[]{:S(2)}) collective-permute-start(bf16[5,256,128]{2,1,0:T(8,128)(2,1)S(1)} %copy-done.5), channel_id=1, source_target_pairs={{8,16},{12,20},{16,8},{20,12},{9,17},{13,21},{17,9},{21,13},{10,18... | collective-permute-start | bytes 983048 | tf_op jit(solution)/shard_map/cond/branch_0_fun/ppermute | solution.py:209
  62.6 14.8 %collective-permute-start.52 = (bf16[5,256,128]{2,1,0:T(8,128)(2,1)S(1)}, bf16[5,256,128]{2,1,0:T(8,128)(2,1)S(1)}, u32[]{:S(2)}, u32[]{:S(2)}) collective-permute-start(bf16[5,256,128]{2,1,0:T(8,128)(2,1)S(1)} %collective-permute-done.49.refs_0_), channel_id=1, source_target_pairs={{8,0},{12,4},{16,24},{20,28},{9,1},{13,5},{17,25},{21,29},{10,2},{... | collective-permute-start | bytes 983048 | tf_op jit(solution)/shard_map/cond/branch_0_fun/ppermute | solution.py:209
  63.9 8.2 %collective-permute-start.50 = (bf16[104,1024]{1,0:T(8,128)(2,1)S(1)}, bf16[104,1024]{1,0:T(8,128)(2,1)S(1)}, u32[]{:S(2)}, u32[]{:S(2)}) collective-permute-start(bf16[104,1024]{1,0:T(8,128)(2,1)S(1)} %get-tuple-element.327), channel_id=1, source_target_pairs={{0,4},{4,0},{8,12},{12,8},{16,20},{20,16},{24,28},{28,24},{1,5},{5... | collective-permute-start | bytes 638984 | tf_op jit(solution)/shard_map/cond/branch_0_fun/ppermute | solution.py:212
  65.7 13.5 %collective-permute-start.53 = (bf16[104,1024]{1,0:T(8,128)(2,1)S(1)}, bf16[104,1024]{1,0:T(8,128)(2,1)S(1)}, u32[]{:S(2)}, u32[]{:S(2)}) collective-permute-start(bf16[104,1024]{1,0:T(8,128)(2,1)S(1)} %get-tuple-element.331), channel_id=1, source_target_pairs={{0,4},{4,0},{8,12},{12,8},{16,20},{20,16},{24,28},{28,24},{1,5},{5... | collective-permute-start | bytes 638984 | tf_op jit(solution)/shard_map/cond/branch_0_fun/ppermute | solution.py:212
  78.6 6.5 %collective-permute-start.54 = (bf16[104,1024]{1,0:T(8,128)(2,1)S(1)}, bf16[104,1024]{1,0:T(8,128)(2,1)S(1)}, u32[]{:S(2)}, u32[]{:S(2)}) collective-permute-start(bf16[104,1024]{1,0:T(8,128)(2,1)S(1)} %get-tuple-element.332), channel_id=1, source_target_pairs={{0,4},{4,0},{8,12},{12,8},{16,20},{20,16},{24,28},{28,24},{1,5},{5... | collective-permute-start | bytes 638984 | tf_op jit(solution)/shard_map/cond/branch_0_fun/ppermute | solution.py:212
